TPU v7x, 32 devices: a whole 2x2x4 slice. The times are simulated.
32 devices in a mesh: flux: 4 (over z), obs: 8 (over y, x, core).
Axes of the slice: x: 2, y: 2, z: 4, core: 2. Of those that a mesh axis runs over, the one named last changes fastest.
Arguments:
- footprint: bfloat16 [256, 4, 4, 2, 4096], P(('flux', 'obs')), may hold values from 0.00049972534 to 0.049804688
- obs_hour: int32 [256, 4], P(('flux', 'obs')), may hold values from 0 to 3
- tile_list: int32 [256, 4], P(('flux', 'obs')), may hold values from 0 to 511, as said below
- tile_row: int32 [512], replicated, may hold values from 0 to 511, as said below
- flux: bfloat16 [512, 5, 4096], P('flux'), may hold values from -6 to 6
- observed: float32 [256, 4], P(('flux', 'obs')), may hold values from -18 to 18
- obs_var: float32 [256, 4], P(('flux', 'obs')), may hold values from 0.5 to 4
Outputs:
- modeled: float32 [256, 4], P(('flux', 'obs'))
- gradient: float32 [512, 5, 4096], P('flux', None, 'obs')
Inputs may be any that keep to these rules, and one draw needn't show every extreme that they name: `tile_row`: A permutation: every tile has its own storage row, and the row r lies on index r // 128 of flux. `tile_list`: among the 32 listed tiles of one device's 8 blocks, at most 16 have storage rows on one index of flux; on every device some index of flux gets exactly 16.
All inputs are finite; a program needn't handle non-finite values.
Results may differ from a plain program's by a relative error of at most 0.0019.
Values may be sent and summed in bfloat16 or wider, within the bound.
No kernel may reach another device: no remote copies, remote signals or barrier semaphores. Data moves between devices by JAX's collectives and lax.ppermute only.
A program may use at most 64 MiB of HBM per device.

v0:
```python
import functools

import jax
import jax.numpy as jnp
from jax import lax
from jax.experimental import pallas as pl
from jax.experimental.pallas import tpu as pltpu
from jax.sharding import PartitionSpec as P

LANES = 128
VMEM_BYTES = 48 * 1024 * 1024
BASE = 8
REST = (0, 2, 8)


def iota(shape, dim):
    return lax.broadcasted_iota(jnp.int32, shape, dim)


def thirds(value):
    high = value.astype(jnp.bfloat16).astype(jnp.float32)
    rest = value - high
    middle = rest.astype(jnp.bfloat16).astype(jnp.float32)
    return high, middle, (rest - middle).astype(jnp.bfloat16).astype(jnp.float32)


class Sizes:
    def __init__(self, owners, columns, footprint, flux):
        self.owners, self.columns = owners, columns
        self.devices = owners * columns
        self.blocks, self.width, self.soundings, self.lags, cells = footprint
        self.tiles, self.hours = flux[0], flux[1]
        self.span = self.hours - self.lags + 1
        self.half = self.span * self.tiles // 2
        self.slots = self.blocks * self.width
        self.per_slot = self.soundings * self.lags
        self.part = cells // columns
        self.lane_tiles = self.part // LANES
        self.first = self.slots // owners
        self.rows = self.first * self.per_slot
        self.spill = self.slots // 2 * self.per_slot
        self.second = columns * self.first * self.per_slot
        self.base = self.second * BASE // 16
        self.notes = 8 * (self.second // self.part)
        self.states = self.blocks * self.soundings
        self.per_page = 8 * LANES // self.states
        self.pages = self.devices // self.per_page


def read_notes(sizes, notes, plane):
    lane = iota((1, notes.shape[1]), 1)
    inner = lax.rem(lane, jnp.int32(sizes.per_slot))
    base = notes[0:1]
    target = (base + sizes.half).astype(jnp.int32) + lax.rem(inner, jnp.int32(sizes.lags)) * sizes.tiles
    target = jnp.where(base > sizes.half - 0.5, -1, target)
    place = notes[1:2].astype(jnp.int32)
    block = lax.rem(place, jnp.int32(sizes.blocks))
    device = plane * sizes.columns + lax.div(place, jnp.int32(sizes.blocks))
    state = block * sizes.soundings + lax.div(inner, jnp.int32(sizes.lags))
    row = lax.div(device, jnp.int32(sizes.per_page)) * 8 + lax.rem(state, jnp.int32(8))
    column = lax.div(state, jnp.int32(8)) * sizes.per_page + lax.rem(device, jnp.int32(sizes.per_page))
    return target, row, column


def first_round(sizes, ref, step):
    sources, count = ref.shape[0], sizes.rows
    feet = jnp.concatenate(
        [
            ref[:, n * count : (n + 1) * count, :].reshape(sources * count, LANES)
            for n in range(sizes.lane_tiles)
        ],
        axis=1,
    )
    end = sizes.lane_tiles * count
    notes = jnp.concatenate(
        [ref[s, end : end + 8, :].astype(jnp.float32)[:, :count] for s in range(sources)], axis=1
    )
    lane = iota((1, sources * count), 1)
    plane = lax.div(step * sources + lax.div(lane, jnp.int32(count)), jnp.int32(sizes.columns))
    return feet, notes, plane


def second_round(sizes, flux_index, bases, rests, with_bases=True):
    notes = [
        jnp.concatenate(
            [ref[n * 8 : (n + 1) * 8, :].astype(jnp.float32) for n in range(sizes.notes // 8)],
            axis=1,
        )
        for ref in bases
    ]
    feet, kept, planes = [], [], []
    if with_bases:
        feet += [ref[sizes.notes :, :] for ref in bases]
        kept += [each[:, : sizes.base] for each in notes]
        planes.append(lax.div(iota((1, len(bases) * sizes.base), 1), jnp.int32(sizes.base)))
    if rests:
        more = rests[0].shape[0]
        feet += [ref[...] for ref in rests]
        kept += [each[:, sizes.base : sizes.base + more] for each in notes]
        planes.append(lax.div(iota((1, len(rests) * more), 1), jnp.int32(more)))
    plane = lax.bitwise_xor(jnp.concatenate(planes, axis=1), flux_index)
    return jnp.concatenate(feet, axis=0), jnp.concatenate(kept, axis=1), plane


def partial_sums(sizes, flux_ref, feet, notes, plane):
    target, row, column = read_notes(sizes, notes, plane)
    count = feet.shape[0]
    levels = sizes.hours * sizes.tiles
    products = lax.dot_general(
        flux_ref[...].reshape(levels, sizes.part),
        feet,
        (((1,), (1,)), ((), ())),
        preferred_element_type=jnp.float32,
    )
    chosen = jnp.where(iota((levels, count), 0) == target, products, 0.0)
    partial = jnp.sum(chosen, axis=0, keepdims=True)
    height = 8 * sizes.pages
    spread = jnp.where(iota((height, count), 0) == row, partial, 0.0)
    terms = jnp.concatenate(thirds(spread), axis=0).astype(jnp.bfloat16)
    lanes = (iota((LANES, count), 0) == column).astype(jnp.bfloat16)
    sums = lax.dot_general(
        terms, lanes, (((1,), (1,)), ((), ())), preferred_element_type=jnp.float32
    )
    return sums[:height] + sums[height : 2 * height] + sums[2 * height :]


def gradient_terms(sizes, model, feet, notes, plane):
    target, row, column = read_notes(sizes, notes, plane)
    count = feet.shape[0]
    height = 8 * sizes.pages
    lanes = (iota((LANES, count), 0) == column).astype(jnp.bfloat16)
    taken = jnp.dot(model, lanes, preferred_element_type=jnp.float32)
    taken = taken[:height] + taken[height : 2 * height] + taken[2 * height :]
    value = jnp.sum(
        jnp.where(iota((height, count), 0) == row, taken, 0.0), axis=0, keepdims=True
    )
    seen = notes[2:3] + notes[3:4] + notes[4:5]
    spread = notes[5:6] + notes[6:7] + notes[7:8]
    scaled = ((value - seen) / spread).astype(jnp.bfloat16).astype(jnp.float32)
    levels = sizes.hours * sizes.tiles
    coefficient = jnp.where(iota((levels, count), 0) == target, scaled, 0.0).astype(jnp.bfloat16)
    return jnp.dot(coefficient, feet, preferred_element_type=jnp.float32)


def pack_kernel(
    sizes, at_ref, list_ref, row_ref, hour_ref, seen_ref, var_ref, feet_ref, send_ref, *rest
):
    spills = rest[: sizes.columns]
    place, first_notes, spill_notes, count = rest[sizes.columns :]
    owners, per_slot = sizes.owners, sizes.per_slot
    step = pl.program_id(0)

    @pl.when(step == 0)
    def _():
        field, lane = iota((16, LANES), 0), iota((16, LANES), 1)
        inner = lane % per_slot
        sounding = inner // sizes.lags
        slot_at = lane // per_slot
        key_at = iota((1, sizes.slots * per_slot), 1)
        key = jnp.zeros(key_at.shape, jnp.int32)
        empty = jnp.where(field == 0, jnp.float32(sizes.half), 0.0)
        empty = jnp.where(field == 5, 1.0, jnp.where(field == 8, -1.0, empty))
        for o in range(owners):
            count[o] = 0
            first_notes[o] = empty[:8]
        count[owners] = 0
        left = empty
        for b in range(sizes.blocks):
            base = jnp.zeros(field.shape, jnp.float32)
            seen = jnp.zeros(field.shape, jnp.float32)
            spread = jnp.ones(field.shape, jnp.float32)
            for o in range(sizes.soundings):
                here = sounding == o
                hour = hour_ref[o, b] * sizes.tiles - sizes.half
                base = jnp.where(here, hour.astype(jnp.float32), base)
                seen = jnp.where(here, seen_ref[o, b], seen)
                spread = jnp.where(here, var_ref[o, b], spread)
            column = (b + sizes.blocks * at_ref[1]).astype(jnp.float32)
            pattern = jnp.where(field == 0, base, jnp.where(field == 1, column, 0.0))
            for n, term in enumerate(thirds(seen) + thirds(spread)):
                pattern = jnp.where(field == 2 + n, term, pattern)
            for k in range(sizes.width):
                stored = row_ref[list_ref[k, b]]
                owner = lax.div(stored, jnp.int32(sizes.tiles))
                tile = (stored - owner * sizes.tiles).astype(jnp.float32)
                position = count[owner]
                count[owner] = position + 1
                keep = position < sizes.first
                over = count[owners]
                count[owners] = over + jnp.where(keep, 0, 1)
                goes = jnp.where(
                    keep, owner * sizes.first + position, owners * sizes.first + over
                )
                value = jnp.where(field == 0, pattern + tile, pattern)
                value = jnp.where(field == 8, owner.astype(jnp.float32), value)
                value = jnp.where(
                    field == 9, (position - sizes.first).astype(jnp.float32), value
                )
                first_notes[owner] = jnp.where(
                    slot_at[:8] == jnp.where(keep, position, -1), value[:8], first_notes[owner]
                )
                left = jnp.where(slot_at == jnp.where(keep, -1, over), value, left)
                key = jnp.where(
                    key_at // per_slot == b * sizes.width + k,
                    goes * per_slot + key_at % per_slot,
                    key,
                )
        counts = jnp.zeros((8, LANES), jnp.float32)
        for o in range(owners):
            over = jnp.maximum(count[o] - sizes.first, 0).astype(jnp.float32)
            counts = jnp.where(lane[:8] == sizes.rows + o, over, counts)
        for o in range(owners):
            first_notes[o] = jnp.where(lane[:8] < sizes.rows, first_notes[o], counts)
        spill_notes[...] = left
        place[...] = (iota(place.shape, 0) == key).astype(jnp.bfloat16)

    packed = jnp.dot(place[...], feet_ref[...], preferred_element_type=jnp.float32)
    packed = packed.astype(jnp.bfloat16)
    rows = sizes.rows
    end = sizes.lane_tiles * rows
    for o in range(owners):
        for n in range(sizes.lane_tiles):
            send_ref[o, 0, n * rows : (n + 1) * rows, :] = packed[
                o * rows : (o + 1) * rows, n * LANES : (n + 1) * LANES
            ]
        send_ref[o, 0, end : end + 8, :] = first_notes[o].astype(jnp.bfloat16)
    for d in range(sizes.columns):

        @pl.when(step == d)
        def _():
            for n in range(sizes.lane_tiles):
                spills[d][n * sizes.spill : (n + 1) * sizes.spill, :] = packed[
                    owners * rows :, n * LANES : (n + 1) * LANES
                ]
            end = sizes.lane_tiles * sizes.spill
            spills[d][end : end + 16, :] = spill_notes[...].astype(jnp.bfloat16)


def level_of(sizes, ref):
    planes = [
        sum(
            ref[p * sizes.columns + j].astype(jnp.float32) for j in range(sizes.columns)
        )
        for p in range(sizes.owners)
    ]
    counts = functools.reduce(jnp.maximum, planes)[0:1]
    lane = iota(counts.shape, 1)
    counts = jnp.where((lane >= sizes.rows) & (lane < sizes.rows + sizes.owners), counts, 0.0)
    most = jnp.max(counts, axis=1, keepdims=True) * sizes.per_slot
    level = jnp.zeros((1, 1), jnp.int32)
    for n in REST[:-1]:
        level = level + jnp.where(most > sizes.base + sizes.second * n // 16, 1, 0)
    return level


def regroup_kernel(sizes, at_ref, *refs):
    columns, owners, spill = sizes.columns, sizes.owners, sizes.spill
    spills, bases = refs[:columns], refs[columns : columns + owners]
    rests = refs[columns + owners : columns + 2 * owners]
    feet, notes, place = refs[columns + 2 * owners :]
    step = pl.program_id(0)
    owner = at_ref[2] ^ step
    end = sizes.lane_tiles * spill

    @pl.when(step == 0)
    def _():
        for d, ref in enumerate(spills):
            for n in range(sizes.lane_tiles):
                feet[d * spill : (d + 1) * spill, n * LANES : (n + 1) * LANES] = ref[
                    n * spill : (n + 1) * spill, :
                ]
            notes[:, d * spill : (d + 1) * spill] = ref[end : end + 16, :].astype(jnp.float32)

    mine = notes[8:9, :] == owner.astype(jnp.float32)
    total = jnp.zeros((1, 1), jnp.float32)
    keys = []
    for d in range(columns):
        here = mine[:, d * spill : (d + 1) * spill]
        position = total + notes[9:10, d * spill : (d + 1) * spill]
        inner = lax.rem(iota((1, spill), 1), jnp.int32(sizes.per_slot))
        keys.append(
            jnp.where(here, position.astype(jnp.int32) * sizes.per_slot + inner, -1)
        )
        total = total + jnp.sum(
            jnp.where(here, 1.0 / sizes.per_slot, 0.0), axis=1, keepdims=True
        )
    key = jnp.concatenate(keys, axis=1)
    place[...] = (iota(place.shape, 0) == key).astype(jnp.bfloat16)
    sorted_feet = jnp.dot(place[...], feet[...], preferred_element_type=jnp.float32)
    sorted_feet = sorted_feet.astype(jnp.bfloat16)
    moved = lax.dot_general(
        notes[0:8, :].astype(jnp.bfloat16),
        place[...],
        (((1,), (1,)), ((), ())),
        preferred_element_type=jnp.float32,
    )
    field, lane = iota(moved.shape, 0), iota(moved.shape, 1)
    empty = jnp.where(field == 0, jnp.float32(sizes.half), jnp.where(field == 5, 1.0, 0.0))
    moved = jnp.where(lane.astype(jnp.float32) < total * sizes.per_slot, moved, empty)
    moved = moved.astype(jnp.bfloat16)
    for o in range(owners):

        @pl.when(step == o)
        def _():
            for n in range(sizes.notes // 8):
                bases[o][n * 8 : (n + 1) * 8, :] = moved[
                    :, n * sizes.part : (n + 1) * sizes.part
                ]
            bases[o][sizes.notes :, :] = sorted_feet[: sizes.base]
            rests[o][...] = sorted_feet[sizes.base :]


def forward_first_kernel(sizes, at_ref, flux_ref, got_ref, all_ref, out_ref, level_ref):
    step = pl.program_id(0)
    feet, notes, plane = first_round(sizes, got_ref, step)
    sums = partial_sums(sizes, flux_ref, feet, notes, plane)

    @pl.when(step == 0)
    def _():
        out_ref[...] = sums
        level_ref[...] = jnp.broadcast_to(level_of(sizes, all_ref), level_ref.shape)

    @pl.when(step > 0)
    def _():
        out_ref[...] += sums


def forward_second_kernel(sizes, more, at_ref, flux_ref, before_ref, *refs):
    bases, rests, out_ref = refs[: sizes.owners], refs[sizes.owners : -1], refs[-1]
    feet, notes, plane = second_round(sizes, at_ref[2], bases, rests, not more)
    sums = before_ref[0] + partial_sums(sizes, flux_ref, feet, notes, plane)
    out_ref[...] = jnp.broadcast_to(sums[None], out_ref.shape)


def adjoint_kernel(sizes, chunks, at_ref, sums_ref, one_ref, *refs):
    bases, rests = refs[: sizes.owners], refs[sizes.owners : -3]
    modeled_ref, grad_ref, model = refs[-3:]
    step = pl.program_id(0)

    @pl.when(step == 0)
    def _():
        sums = jnp.sum(sums_ref[...], axis=0)
        model[...] = jnp.concatenate(thirds(sums), axis=0).astype(jnp.bfloat16)
        me = at_ref[0]
        page, within = lax.div(me, sizes.per_page), lax.rem(me, sizes.per_page)
        lane = iota((8, LANES), 1)
        own = jnp.zeros((8, LANES), jnp.float32)
        for p in range(sizes.pages):
            own = jnp.where(page == p, sums[p * 8 : (p + 1) * 8], own)
        result = jnp.zeros(modeled_ref.shape, jnp.float32)
        at_block = iota(modeled_ref.shape, 1)
        each = 8 // sizes.soundings
        for q in range(sizes.states // 8):
            picked = jnp.where(lane == q * sizes.per_page + within, own, 0.0)
            column = jnp.sum(picked, axis=1, keepdims=True)
            for n in range(each):
                values = column[n * sizes.soundings : (n + 1) * sizes.soundings]
                result = jnp.where(at_block == q * each + n, values, result)
        modeled_ref[...] = result

    @pl.when(step < chunks)
    def _():
        feet, notes, plane = first_round(sizes, one_ref, step)
        terms = gradient_terms(sizes, model[...], feet, notes, plane).reshape(grad_ref.shape)

        @pl.when(step == 0)
        def _():
            grad_ref[...] = terms

        @pl.when(step > 0)
        def _():
            grad_ref[...] += terms

    @pl.when(step == chunks)
    def _():
        feet, notes, plane = second_round(sizes, at_ref[2], bases, rests)
        terms = gradient_terms(sizes, model[...], feet, notes, plane)
        grad_ref[...] += terms.reshape(grad_ref.shape)


def shards(footprint, obs_hour, tile_list, tile_row, flux, observed, obs_var):
    sizes = Sizes(
        lax.axis_size("flux"), lax.axis_size("obs"), footprint.shape, flux.shape
    )
    owners, columns, devices, part = sizes.owners, sizes.columns, sizes.devices, sizes.part
    both = ("flux", "obs")
    params = pltpu.CompilerParams(vmem_limit_bytes=VMEM_BYTES)
    smem = pl.BlockSpec(memory_space=pltpu.SMEM)
    me = lax.axis_index("flux") * columns + lax.axis_index("obs")
    at = jnp.stack([me, lax.axis_index("obs"), lax.axis_index("flux")])
    flux = flux.transpose(1, 0, 2)

    first_height = sizes.lane_tiles * sizes.rows + 8
    spill_height = sizes.lane_tiles * sizes.spill + 16
    all_slots = sizes.slots * sizes.per_slot
    send, *spills = pl.pallas_call(
        functools.partial(pack_kernel, sizes),
        grid_spec=pltpu.PrefetchScalarGridSpec(
            num_scalar_prefetch=1,
            grid=(columns,),
            in_specs=[smem] * 5
            + [pl.BlockSpec((all_slots, part), lambda d, at: (0, d ^ at[1]))],
            out_specs=[
                pl.BlockSpec((owners, 1, first_height, LANES), lambda d, at: (0, d ^ at[1], 0, 0))
            ]
            + [pl.BlockSpec((spill_height, LANES), lambda d, at: (0, 0))] * columns,
            scratch_shapes=[
                pltpu.VMEM((owners * sizes.rows + sizes.spill, all_slots), jnp.bfloat16),
                pltpu.VMEM((owners, 8, LANES), jnp.float32),
                pltpu.VMEM((16, LANES), jnp.float32),
                pltpu.SMEM((owners + 1,), jnp.int32),
            ],
        ),
        out_shape=[pltpu.HBM((owners, columns, first_height, LANES), jnp.bfloat16)]
        + [jax.ShapeDtypeStruct((spill_height, LANES), jnp.bfloat16)] * columns,
        compiler_params=params,
        name="pack",
    )(
        at,
        tile_list.T,
        tile_row,
        obs_hour.T,
        observed.T,
        obs_var.T,
        footprint.reshape(all_slots, sizes.lane_tiles * columns * LANES),
    )
    got = lax.all_to_all(
        send.reshape(devices, first_height, LANES), both, split_axis=0, concat_axis=0, tiled=True
    )
    spills = spills[:1] + [
        lax.ppermute(spills[d], "obs", [(i, i ^ d) for i in range(columns)])
        for d in range(1, columns)
    ]
    second_height = sizes.notes + sizes.second
    base_height, more_height = sizes.notes + sizes.base, sizes.second - sizes.base
    outs = [(base_height, part)] * owners + [(more_height, part)] * owners
    parts = pl.pallas_call(
        functools.partial(regroup_kernel, sizes),
        grid_spec=pltpu.PrefetchScalarGridSpec(
            num_scalar_prefetch=1,
            grid=(owners,),
            in_specs=[pl.BlockSpec((spill_height, LANES), lambda o, at: (0, 0))] * columns,
            out_specs=[pl.BlockSpec(shape, lambda o, at: (0, 0)) for shape in outs],
            scratch_shapes=[
                pltpu.VMEM((columns * sizes.spill, part), jnp.bfloat16),
                pltpu.VMEM((16, columns * sizes.spill), jnp.float32),
                pltpu.VMEM((sizes.second, columns * sizes.spill), jnp.bfloat16),
            ],
        ),
        out_shape=[jax.ShapeDtypeStruct(shape, jnp.bfloat16) for shape in outs],
        compiler_params=params,
        name="regroup",
    )(at, *spills)

    def swap(arrays):
        return arrays[:1] + [
            lax.ppermute(arrays[n], "flux", [(i, i ^ n) for i in range(owners)])
            for n in range(1, owners)
        ]

    parts = list(parts)
    bases, rests = swap(parts[:owners]), parts[owners:]

    sources = min(devices, 1024 // sizes.rows)
    chunks = devices // sources
    copies = devices if devices <= 64 else 1
    height = 8 * sizes.pages
    flux_spec = pl.BlockSpec((sizes.hours, sizes.tiles, part), lambda i, at: (0, 0, at[1]))
    base_specs = [pl.BlockSpec((base_height, part), lambda i, at: (0, 0))] * owners
    early, level = pl.pallas_call(
        functools.partial(forward_first_kernel, sizes),
        grid_spec=pltpu.PrefetchScalarGridSpec(
            num_scalar_prefetch=1,
            grid=(chunks,),
            in_specs=[
                flux_spec,
                pl.BlockSpec((sources, first_height, LANES), lambda i, at: (i, 0, 0)),
                pl.BlockSpec((devices, 8, LANES), lambda i, at: (0, first_height // 8 - 1, 0)),
            ],
            out_specs=(
                pl.BlockSpec((height, LANES), lambda i, at: (0, 0)),
                pl.BlockSpec((8, LANES), lambda i, at: (0, 0)),
            ),
        ),
        out_shape=(
            jax.ShapeDtypeStruct((height, LANES), jnp.float32),
            jax.ShapeDtypeStruct((8, LANES), jnp.int32),
        ),
        compiler_params=params,
        name="forward_first",
    )(at, flux, got, got)

    def forward_second(flux, before, bases, rests, more):
        return pl.pallas_call(
            functools.partial(forward_second_kernel, sizes, more > 0),
            grid_spec=pltpu.PrefetchScalarGridSpec(
                num_scalar_prefetch=1,
                grid=(1,),
                in_specs=[flux_spec, pl.BlockSpec((1, height, LANES), lambda i, at: (0, 0, 0))]
                + base_specs
                + [pl.BlockSpec((more, part), lambda i, at: (0, 0))] * len(rests),
                out_specs=pl.BlockSpec((copies, height, LANES), lambda i, at: (0, 0, 0)),
            ),
            out_shape=jax.ShapeDtypeStruct((copies, height, LANES), jnp.float32),
            compiler_params=params,
            name="forward_more" if more else "forward_second",
        )(at, flux, before, *bases, *rests)

    sums = forward_second(flux, early[None], bases, [], 0)

    def finish(sixteenths):
        more = sizes.second * sixteenths // 16

        def run(flux, got, sums, bases, rests, at):
            if more:
                rests = rests[:1] + swap([rest[:more] for rest in rests])[1:]
                sums = forward_second(flux, sums, bases, rests, more)
            else:
                rests = []
            if copies > 1:
                sums = lax.all_to_all(sums, both, split_axis=0, concat_axis=0, tiled=True)
            else:
                sums = lax.psum(sums, both)
            return pl.pallas_call(
                functools.partial(adjoint_kernel, sizes, chunks),
                grid_spec=pltpu.PrefetchScalarGridSpec(
                    num_scalar_prefetch=1,
                    grid=(chunks + 1,),
                    in_specs=[
                        pl.BlockSpec((copies, height, LANES), lambda i, at: (0, 0, 0)),
                        pl.BlockSpec(
                            (sources, first_height, LANES),
                            lambda i, at: (jnp.minimum(i, chunks - 1), 0, 0),
                        ),
                    ]
                    + base_specs
                    + [pl.BlockSpec((more, part), lambda i, at: (0, 0))] * len(rests),
                    out_specs=(
                        pl.BlockSpec((sizes.soundings, sizes.blocks), lambda i, at: (0, 0)),
                        pl.BlockSpec((sizes.hours, sizes.tiles, part), lambda i, at: (0, 0, 0)),
                    ),
                    scratch_shapes=[pltpu.VMEM((3 * height, LANES), jnp.bfloat16)],
                ),
                out_shape=(
                    jax.ShapeDtypeStruct((sizes.soundings, sizes.blocks), jnp.float32),
                    jax.ShapeDtypeStruct((sizes.hours, sizes.tiles, part), jnp.float32),
                ),
                compiler_params=params,
                name="adjoint",
            )(at, sums, got, *bases, *rests)

        return run

    modeled, gradient = lax.switch(
        level[0, 0], [finish(n) for n in REST], flux, got, sums, bases, rests, at
    )
    return modeled.T, gradient.transpose(1, 0, 2)


def solution(mesh):
    placed = (
        P(("flux", "obs"), None, None, None, None),
        P(("flux", "obs"), None),
        P(("flux", "obs"), None),
        P(),
        P("flux", None, None),
        P(("flux", "obs"), None),
        P(("flux", "obs"), None),
    )
    return jax.shard_map(
        shards,
        mesh=mesh,
        in_specs=placed,
        out_specs=(P(("flux", "obs"), None), P("flux", None, "obs")),
        check_vma=False,
    )
```

profile of v0, /device:TPU:0, one launch (start us, length us, event | category | flops | bytes accessed | tf_op | source)
XLA Modules:
  0.0 111.4 jit_solution(4438039331757392938)
XLA Ops:
  0.6 0.0 copy-start
  0.6 0.0 copy-start.1
  0.7 0.0 copy-start.2
  0.7 0.0 copy-start.3
  0.7 0.0 copy-start.4
  0.7 2.8 %reshape.13.feet_ref = bf16[256,4096]{1,0:T(8,128)(2,1)S(1)} reshape(bf16[8,4,4,2,4096]{4,3,2,1,0:T(2,128)(2,1)} %param.10) | data formatting | bytes 4194304 | tf_op jit(solution)/shard_map/reshape | solution.py:425
  3.5 0.1 pad_add_fusion.at_ref
  3.6 0.0 copy-done
  3.6 0.0 copy-done.1
  3.6 0.0 copy-done.2
  3.6 0.0 copy-done.3
  3.6 0.0 copy-done.4
  3.6 6.5 %pack.1 = (bf16[4,8,264,128]{3,2,1,0:T(8,128)(2,1)}, bf16[528,128]{1,0:T(8,128)(2,1)S(1)}, bf16[528,128]{1,0:T(8,128)(2,1)S(1)}, bf16[528,128]{1,0:T(8,128)(2,1)...) custom-call(s32[3]{0:T(128)S(1)} %pad_add_fusion.at_ref, ...), custom_call_target="tpu_custom_call" | custom-call | tf_op jit(solution)/shard_map/pack/pallas_call | solution.py:396
  10.1 7.3 %all-to-all-start.3 = ((bf16[32,264,128]{2,1,0:T(8,128)(2,1)}), bf16[32,264,128]{2,1,0:T(8,128)(2,1)S(1)}, u32[]{:S(2)}, u32[]{:S(2)}) async-start(bf16[32,264,128]{2,1,0:T(8,128)(2,1)} %bitcast.22), calls=%async_computation.3 | async-start | bytes 4325376 | tf_op jit(solution)/shard_map/all_to_all | solution.py:427
  17.3 0.3 collective-permute-start.6
  17.6 1.7 %collective-permute-start.7 = (bf16[528,128]{1,0:T(8,128)(2,1)S(1)}, bf16[528,128]{1,0:T(8,128)(2,1)S(1)}, u32[]{:S(2)}, u32[]{:S(2)}) collective-permute-start(bf16[528,128]{1,0:T(8,128)(2,1)S(1)} %get-tuple-element.121), channel_id=1, source_target_pairs={{0,2},{1,3},{2,0},{3,1},{4,6},{5,7},{6,4},{7,5},{8,10},{9,11},{10,... | collective-permute-start | bytes 405512 | tf_op jit(solution)/shard_map/ppermute | solution.py:431
  19.3 0.0 collective-permute-start.8
  19.3 1.7 %collective-permute-start.9 = (bf16[528,128]{1,0:T(8,128)(2,1)S(1)}, bf16[528,128]{1,0:T(8,128)(2,1)S(1)}, u32[]{:S(2)}, u32[]{:S(2)}) collective-permute-start(bf16[528,128]{1,0:T(8,128)(2,1)S(1)} %get-tuple-element.123), channel_id=1, source_target_pairs={{0,4},{1,5},{2,6},{3,7},{4,0},{5,1},{6,2},{7,3},{8,12},{9,13},{10,... | collective-permute-start | bytes 405512 | tf_op jit(solution)/shard_map/ppermute | solution.py:431
  21.0 0.1 collective-permute-start.10
  21.1 0.0 collective-permute-done.6.refs_1_
  21.1 2.6 %collective-permute-start.11 = (bf16[528,128]{1,0:T(8,128)(2,1)S(1)}, bf16[528,128]{1,0:T(8,128)(2,1)S(1)}, u32[]{:S(2)}, u32[]{:S(2)}) collective-permute-start(bf16[528,128]{1,0:T(8,128)(2,1)S(1)} %get-tuple-element.125), channel_id=1, source_target_pairs={{0,6},{1,7},{2,4},{3,5},{4,2},{5,3},{6,0},{7,1},{8,14},{9,15},{10,... | collective-permute-start | bytes 405512 | tf_op jit(solution)/shard_map/ppermute | solution.py:431
  23.7 13.5 %collective-permute-done.7.refs_2_ = bf16[528,128]{1,0:T(8,128)(2,1)S(1)} collective-permute-done((bf16[528,128]{1,0:T(8,128)(2,1)S(1)}, bf16[528,128]{1,0:T(8,128)(2,1)S(1)}, u32[]{:S(2)}, u32[]{:S(2)}) %collective-permute-start.7) | collective-permute-done | bytes 135200 | tf_op jit(solution)/shard_map/ppermute | solution.py:431
  37.2 0.3 collective-permute-start.12
  37.5 4.5 %collective-permute-done.8.refs_3_ = bf16[528,128]{1,0:T(8,128)(2,1)S(1)} collective-permute-done((bf16[528,128]{1,0:T(8,128)(2,1)S(1)}, bf16[528,128]{1,0:T(8,128)(2,1)S(1)}, u32[]{:S(2)}, u32[]{:S(2)}) %collective-permute-start.8) | collective-permute-done | bytes 135200 | tf_op jit(solution)/shard_map/ppermute | solution.py:431
  42.1 0.0 collective-permute-done.9.refs_4_
  42.1 0.0 collective-permute-done.10.refs_5_
  42.1 8.3 %collective-permute-done.11.refs_6_ = bf16[528,128]{1,0:T(8,128)(2,1)S(1)} collective-permute-done((bf16[528,128]{1,0:T(8,128)(2,1)S(1)}, bf16[528,128]{1,0:T(8,128)(2,1)S(1)}, u32[]{:S(2)}, u32[]{:S(2)}) %collective-permute-start.11) | collective-permute-done | bytes 135200 | tf_op jit(solution)/shard_map/ppermute | solution.py:431
  50.3 2.2 %collective-permute-done.12.refs_7_ = bf16[528,128]{1,0:T(8,128)(2,1)S(1)} collective-permute-done((bf16[528,128]{1,0:T(8,128)(2,1)S(1)}, bf16[528,128]{1,0:T(8,128)(2,1)S(1)}, u32[]{:S(2)}, u32[]{:S(2)}) %collective-permute-start.12) | collective-permute-done | bytes 135200 | tf_op jit(solution)/shard_map/ppermute | solution.py:431
  52.6 5.8 %regroup.1 = (bf16[264,512]{1,0:T(8,128)(2,1)S(1)}, bf16[264,512]{1,0:T(8,128)(2,1)S(1)}, bf16[264,512]{1,0:T(8,128)(2,1)S(1)}, bf16[264,512]{1,0:T(8,128)(2,1)S...) custom-call(s32[3]{0:T(128)S(1)} %pad_add_fusion.at_ref, ...), custom_call_target="tpu_custom_call" | custom-call | tf_op jit(solution)/shard_map/regroup/pallas_call | solution.py:437
  58.4 0.6 collective-permute-start.13
  59.0 4.2 %collective-permute-start.14 = (bf16[264,512]{1,0:T(8,128)(2,1)S(1)}, bf16[264,512]{1,0:T(8,128)(2,1)}, u32[]{:S(2)}, u32[]{:S(2)}) collective-permute-start(bf16[264,512]{1,0:T(8,128)(2,1)S(1)} %get-tuple-element.129), channel_id=1, source_target_pairs={{0,16},{8,24},{16,0},{24,8},{1,17},{9,25},{17,1},{25,9},{2,18},{10... | collective-permute-start | bytes 811016 | tf_op jit(solution)/shard_map/ppermute | solution.py:457
  63.3 0.0 collective-permute-start.15
  63.3 5.1 %all-to-all-done.3.got_ref.all_ref = bf16[32,264,128]{2,1,0:T(8,128)(2,1)S(1)} async-done(((bf16[32,264,128]{2,1,0:T(8,128)(2,1)}), bf16[32,264,128]{2,1,0:T(8,128)(2,1)S(1)}, u32[]{:S(2)}, u32[]{:S(2)}) %all-to-all-start.3) | async-done | bytes 2162720 | tf_op jit(solution)/shard_map/all_to_all | solution.py:427
  68.4 3.9 %forward_first.1 = (f32[8,128]{1,0:T(8,128)S(1)}, s32[8,128]{1,0:T(8,128)S(1)}) custom-call(s32[3]{0:T(128)S(1)} %pad_add_fusion.at_ref, bf16[5,128,4096]{2,1,0:T(8,128)(2,1)} %bitcast.18, bf16[32,264,128]{2,1,0:T(8,128)(2,1)S(1)} %all-to-all-done.3.got_ref.all_ref, bf16[32,264,128]{2,1,0:T(8,128)(2,1)S(1)} %all-to-all-done.3.got_ref.all_ref), custom_call_target="tpu_custom_call" | custom-call | tf_op jit(solution)/shard_map/forward_first/pallas_call | solution.py:470
  72.3 0.5 slice.12
  73.4 0.0 collective-permute-done.13.refs_1_
  73.5 12.4 %collective-permute-done.14.refs_2_ = bf16[264,512]{1,0:T(8,128)(2,1)} collective-permute-done((bf16[264,512]{1,0:T(8,128)(2,1)S(1)}, bf16[264,512]{1,0:T(8,128)(2,1)}, u32[]{:S(2)}, u32[]{:S(2)}) %collective-permute-start.14) | collective-permute-done | bytes 270368 | tf_op jit(solution)/shard_map/ppermute | solution.py:457
  85.8 0.0 collective-permute-done.15.refs_3_
  85.8 0.0 copy-start.5
  85.8 0.0 copy-start.6
  85.8 0.0 copy-start.7
  85.8 0.0 copy-start.8
  85.8 3.0 %forward_second.1 = f32[32,8,128]{2,1,0:T(8,128)S(1)} custom-call(s32[3]{0:T(128)S(1)} %pad_add_fusion.at_ref, bf16[5,128,4096]{2,1,0:T(8,128)(2,1)} %bitcast.19, f32[1,8,128]{2,1,0:T(8,128)S(1)} %bitcast.13, bf16[264,512]{1,0:T(8,128)(2,1)S(1)} %get-tuple-element.127.refs_0_, bf16[264,512]{1,0:T(8,128)(2,1)} %collective-permute-done.13.refs_1_, ...), custom_call_target="tpu_custom_call" | custom-call | tf_op jit(solution)/shard_map/forward_second/pallas_call | solution.py:494
  88.8 0.0 copy-done.5
  88.8 0.0 copy-done.6
  88.8 0.0 copy-done.7
  88.8 0.0 copy-done.8
  88.8 22.5 %conditional.1 = ((f32[4,8]{1,0:T(4,128)}, f32[5,128,512]{2,1,0:T(8,128)})) conditional(s32[]{:T(128)} %bitcast.9, (f32[32,8,128]{2,1,0:T(8,128)S(1)}, s32[3]{0:T(128)S(1)}, bf16[32,264,128]{2,1,0:T(8,128)(2,1)S(1)}, bf16[264,512]{1,0:T(8,128)(2,1)S(1)}, bf16[264,512]{1,0:T(8,128)(2,1)}, /*index=5*/bf16[264,512]{1,0:T(8,128)(2,1)}, ...), branch_computations={%region_0.0_spmd, %region_1.0_spmd, %region_2.0_spmd} | conditional | bytes 3408000 | solution.py:554
  88.8 16.3 %all_to_all.17.sums_ref = f32[32,8,128]{2,1,0:T(8,128)S(1)} all-to-all(f32[32,8,128]{2,1,0:T(8,128)S(1)} %get-tuple-element.63), channel_id=1, replica_groups=mesh['flux'=4,'obs'=8] {'flux','obs'}, dimensions={0} | all-to-all | bytes 262144 | tf_op jit(solution)/shard_map/cond/branch_0_fun/all_to_all | solution.py:521
  105.1 6.2 %adjoint.3 = (f32[4,8]{1,0:T(4,128)}, f32[5,128,512]{2,1,0:T(8,128)}) custom-call(s32[3]{0:T(128)S(1)} %get-tuple-element.62.at_ref, f32[32,8,128]{2,1,0:T(8,128)S(1)} %all_to_all.17.sums_ref, bf16[32,264,128]{2,1,0:T(8,128)(2,1)S(1)} %get-tuple-element.64.one_ref, bf16[264,512]{1,0:T(8,128)(2,1)S(1)} %get-tuple-element.65.refs_0_, ...), custom_call_target="tpu_custom_call" | custom-call | tf_op jit(solution)/shard_map/cond/branch_0_fun/adjoint/pallas_call | solution.py:524
Async XLA Ops:
  0.6 2.9 %copy-start = (s32[8,4]{0,1:T(4,128)S(1)}, s32[8,4]{0,1:T(4,128)}, u32[]{:S(2)}) copy-start(s32[8,4]{0,1:T(4,128)} %param.12) | copy-start | bytes 388
  0.6 2.9 %copy-start.1 = (s32[512]{0:T(512)S(1)}, s32[512]{0:T(512)}, u32[]{:S(2)}) copy-start(s32[512]{0:T(512)} %row_ref.1) | copy-start | bytes 6148
  0.7 2.9 %copy-start.2 = (s32[8,4]{0,1:T(4,128)S(1)}, s32[8,4]{0,1:T(4,128)}, u32[]{:S(2)}) copy-start(s32[8,4]{0,1:T(4,128)} %param.11) | copy-start | bytes 388
  0.7 2.9 %copy-start.3 = (f32[8,4]{0,1:T(4,128)S(1)}, f32[8,4]{0,1:T(4,128)}, u32[]{:S(2)}) copy-start(f32[8,4]{0,1:T(4,128)} %param.15) | copy-start | bytes 388
  0.7 2.9 %copy-start.4 = (f32[8,4]{0,1:T(4,128)S(1)}, f32[8,4]{0,1:T(4,128)}, u32[]{:S(2)}) copy-start(f32[8,4]{0,1:T(4,128)} %param.16) | copy-start | bytes 388
  10.1 58.3 %all-to-all-start.3 = ((bf16[32,264,128]{2,1,0:T(8,128)(2,1)}), bf16[32,264,128]{2,1,0:T(8,128)(2,1)S(1)}, u32[]{:S(2)}, u32[]{:S(2)}) async-start(bf16[32,264,128]{2,1,0:T(8,128)(2,1)} %bitcast.22), calls=%async_computation.3 | async-start | bytes 4325376 | tf_op jit(solution)/shard_map/all_to_all | solution.py:427
  17.3 3.8 %collective-permute-start.6 = (bf16[528,128]{1,0:T(8,128)(2,1)S(1)}, bf16[528,128]{1,0:T(8,128)(2,1)S(1)}, u32[]{:S(2)}, u32[]{:S(2)}) collective-permute-start(bf16[528,128]{1,0:T(8,128)(2,1)S(1)} %get-tuple-element.120), channel_id=1, source_target_pairs={{0,1},{1,0},{2,3},{3,2},{4,5},{5,4},{6,7},{7,6},{8,9},{9,8},{10,11... | collective-permute-start | bytes 405512 | tf_op jit(solution)/shard_map/ppermute | solution.py:431
  17.6 19.6 %collective-permute-start.7 = (bf16[528,128]{1,0:T(8,128)(2,1)S(1)}, bf16[528,128]{1,0:T(8,128)(2,1)S(1)}, u32[]{:S(2)}, u32[]{:S(2)}) collective-permute-start(bf16[528,128]{1,0:T(8,128)(2,1)S(1)} %get-tuple-element.121), channel_id=1, source_target_pairs={{0,2},{1,3},{2,0},{3,1},{4,6},{5,7},{6,4},{7,5},{8,10},{9,11},{10,... | collective-permute-start | bytes 405512 | tf_op jit(solution)/shard_map/ppermute | solution.py:431
  19.3 22.8 %collective-permute-start.8 = (bf16[528,128]{1,0:T(8,128)(2,1)S(1)}, bf16[528,128]{1,0:T(8,128)(2,1)S(1)}, u32[]{:S(2)}, u32[]{:S(2)}) collective-permute-start(bf16[528,128]{1,0:T(8,128)(2,1)S(1)} %get-tuple-element.122), channel_id=1, source_target_pairs={{0,3},{1,2},{2,1},{3,0},{4,7},{5,6},{6,5},{7,4},{8,11},{9,10},{10,... | collective-permute-start | bytes 405512 | tf_op jit(solution)/shard_map/ppermute | solution.py:431
  19.3 22.8 %collective-permute-start.9 = (bf16[528,128]{1,0:T(8,128)(2,1)S(1)}, bf16[528,128]{1,0:T(8,128)(2,1)S(1)}, u32[]{:S(2)}, u32[]{:S(2)}) collective-permute-start(bf16[528,128]{1,0:T(8,128)(2,1)S(1)} %get-tuple-element.123), channel_id=1, source_target_pairs={{0,4},{1,5},{2,6},{3,7},{4,0},{5,1},{6,2},{7,3},{8,12},{9,13},{10,... | collective-permute-start | bytes 405512 | tf_op jit(solution)/shard_map/ppermute | solution.py:431
  21.0 21.1 %collective-permute-start.10 = (bf16[528,128]{1,0:T(8,128)(2,1)S(1)}, bf16[528,128]{1,0:T(8,128)(2,1)S(1)}, u32[]{:S(2)}, u32[]{:S(2)}) collective-permute-start(bf16[528,128]{1,0:T(8,128)(2,1)S(1)} %get-tuple-element.124), channel_id=1, source_target_pairs={{0,5},{1,4},{2,7},{3,6},{4,1},{5,0},{6,3},{7,2},{8,13},{9,12},{10,... | collective-permute-start | bytes 405512 | tf_op jit(solution)/shard_map/ppermute | solution.py:431
  21.1 29.2 %collective-permute-start.11 = (bf16[528,128]{1,0:T(8,128)(2,1)S(1)}, bf16[528,128]{1,0:T(8,128)(2,1)S(1)}, u32[]{:S(2)}, u32[]{:S(2)}) collective-permute-start(bf16[528,128]{1,0:T(8,128)(2,1)S(1)} %get-tuple-element.125), channel_id=1, source_target_pairs={{0,6},{1,7},{2,4},{3,5},{4,2},{5,3},{6,0},{7,1},{8,14},{9,15},{10,... | collective-permute-start | bytes 405512 | tf_op jit(solution)/shard_map/ppermute | solution.py:431
  37.2 15.4 %collective-permute-start.12 = (bf16[528,128]{1,0:T(8,128)(2,1)S(1)}, bf16[528,128]{1,0:T(8,128)(2,1)S(1)}, u32[]{:S(2)}, u32[]{:S(2)}) collective-permute-start(bf16[528,128]{1,0:T(8,128)(2,1)S(1)} %get-tuple-element.126), channel_id=1, source_target_pairs={{0,7},{1,6},{2,5},{3,4},{4,3},{5,2},{6,1},{7,0},{8,15},{9,14},{10,... | collective-permute-start | bytes 405512 | tf_op jit(solution)/shard_map/ppermute | solution.py:431
  58.4 15.0 %collective-permute-start.13 = (bf16[264,512]{1,0:T(8,128)(2,1)S(1)}, bf16[264,512]{1,0:T(8,128)(2,1)}, u32[]{:S(2)}, u32[]{:S(2)}) collective-permute-start(bf16[264,512]{1,0:T(8,128)(2,1)S(1)} %get-tuple-element.128), channel_id=1, source_target_pairs={{0,8},{8,0},{16,24},{24,16},{1,9},{9,1},{17,25},{25,17},{2,10},{10... | collective-permute-start | bytes 811016 | tf_op jit(solution)/shard_map/ppermute | solution.py:457
  59.0 26.8 %collective-permute-start.14 = (bf16[264,512]{1,0:T(8,128)(2,1)S(1)}, bf16[264,512]{1,0:T(8,128)(2,1)}, u32[]{:S(2)}, u32[]{:S(2)}) collective-permute-start(bf16[264,512]{1,0:T(8,128)(2,1)S(1)} %get-tuple-element.129), channel_id=1, source_target_pairs={{0,16},{8,24},{16,0},{24,8},{1,17},{9,25},{17,1},{25,9},{2,18},{10... | collective-permute-start | bytes 811016 | tf_op jit(solution)/shard_map/ppermute | solution.py:457
  63.3 22.5 %collective-permute-start.15 = (bf16[264,512]{1,0:T(8,128)(2,1)S(1)}, bf16[264,512]{1,0:T(8,128)(2,1)}, u32[]{:S(2)}, u32[]{:S(2)}) collective-permute-start(bf16[264,512]{1,0:T(8,128)(2,1)S(1)} %get-tuple-element.130), channel_id=1, source_target_pairs={{0,24},{8,16},{16,8},{24,0},{1,25},{9,17},{17,9},{25,1},{2,26},{10... | collective-permute-start | bytes 811016 | tf_op jit(solution)/shard_map/ppermute | solution.py:457
  85.8 3.0 %copy-start.5 = (bf16[256,512]{1,0:T(8,128)(2,1)S(1)}, bf16[256,512]{1,0:T(8,128)(2,1)}, u32[]{:S(2)}) copy-start(bf16[256,512]{1,0:T(8,128)(2,1)} %get-tuple-element.134) | copy-start | bytes 786436
  85.8 3.0 %copy-start.6 = (bf16[256,512]{1,0:T(8,128)(2,1)S(1)}, bf16[256,512]{1,0:T(8,128)(2,1)}, u32[]{:S(2)}) copy-start(bf16[256,512]{1,0:T(8,128)(2,1)} %get-tuple-element.131) | copy-start | bytes 786436
  85.8 3.0 %copy-start.7 = (bf16[256,512]{1,0:T(8,128)(2,1)S(1)}, bf16[256,512]{1,0:T(8,128)(2,1)}, u32[]{:S(2)}) copy-start(bf16[256,512]{1,0:T(8,128)(2,1)} %get-tuple-element.132) | copy-start | bytes 786436
  85.8 3.0 %copy-start.8 = (bf16[256,512]{1,0:T(8,128)(2,1)S(1)}, bf16[256,512]{1,0:T(8,128)(2,1)}, u32[]{:S(2)}) copy-start(bf16[256,512]{1,0:T(8,128)(2,1)} %get-tuple-element.133) | copy-start | bytes 786436
where the time goes:
time: 112 us; the launch traced here: 111 us
  waiting for transfers between devices  46 us (41%)
  Pallas kernels  25.4 us (23%)
  starting transfers between devices  18.8 us (17%)
  blocking collectives  16.3 us (15%)
  local copies, waits for them, and re-layouts  3.35 us (3%)
  between operations  1.45 us (1%)
    ppermute x7, waiting for transfers between devices, shards(): lax.ppermute(spills[d], 'obs', [(i, i ^ d) for i in range(columns)])  28.5 us
    all_to_all x1, blocking collectives, run(): sums = lax.all_to_all(sums, both, split_axis=0, concat_axis=0, tiled=True)  16.3 us
    ppermute x3, waiting for transfers between devices, swap(): lax.ppermute(arrays[n], 'flux', [(i, i ^ n) for i in range(owners)])  12.4 us
    all_to_all x1, starting transfers between devices, shards(): lax.all_to_all(send.reshape(devices, first_height, LANES), both, split_ax...  7.25 us
    ppermute x7, starting transfers between devices, shards(): lax.ppermute(spills[d], 'obs', [(i, i ^ d) for i in range(columns)])  6.71 us
    pallas_call x1, Pallas kernels, shards(): pl.pallas_call(functools.partial(pack_kernel, sizes), grid_spec=pltpu.Pre...  6.49 us
    pallas_call x1, Pallas kernels, run(): pl.pallas_call(functools.partial(adjoint_kernel, sizes, chunks), grid_spe...  6.22 us
    pallas_call x1, Pallas kernels, shards(): pl.pallas_call(functools.partial(regroup_kernel, sizes), grid_spec=pltpu....  5.84 us
  transfers between devices with their start and end apart: 11, of which 6 were waited for; matrix products, arithmetic and copies ran while one was open for 0% of the time, Pallas kernels for 9%

commit v1 on v0

--- a/solution.py
+++ b/solution.py
@@ -9,8 +9,10 @@
 
 LANES = 128
 VMEM_BYTES = 48 * 1024 * 1024
+ALL_VMEM_BYTES = 60 * 1024 * 1024
 BASE = 8
 REST = (0, 2, 8)
+PACK_STEPS = 2
 
 
 def iota(shape, dim):
@@ -142,16 +144,25 @@
     return jnp.dot(coefficient, feet, preferred_element_type=jnp.float32)
 
 
-def pack_kernel(
-    sizes, at_ref, list_ref, row_ref, hour_ref, seen_ref, var_ref, feet_ref, send_ref, *rest
-):
-    spills = rest[: sizes.columns]
-    place, first_notes, spill_notes, count = rest[sizes.columns :]
+def pack_kernel(sizes, at_ref, *refs):
+    tables, feet_ref, send_ref = refs[:5], refs[5], refs[6]
+    spills = refs[7 : 7 + sizes.columns]
+    place, first_notes, spill_notes, over_rows, count, *local, arrived = refs[7 + sizes.columns :]
+    list_ref, row_ref, hour_ref, seen_ref, var_ref = local
     owners, per_slot = sizes.owners, sizes.per_slot
     step = pl.program_id(0)
+    group = sizes.columns // PACK_STEPS
 
     @pl.when(step == 0)
     def _():
+        copies = [
+            pltpu.make_async_copy(table, here, arrived.at[n])
+            for n, (table, here) in enumerate(zip(tables, local))
+        ]
+        for copy in copies:
+            copy.start()
+        for copy in copies:
+            copy.wait()
         field, lane = iota((16, LANES), 0), iota((16, LANES), 1)
         inner = lane % per_slot
         sounding = inner // sizes.lags
@@ -214,26 +225,28 @@
         spill_notes[...] = left
         place[...] = (iota(place.shape, 0) == key).astype(jnp.bfloat16)
 
-    packed = jnp.dot(place[...], feet_ref[...], preferred_element_type=jnp.float32)
+    feet = feet_ref[...].reshape(place.shape[1], group * sizes.part)
+    packed = jnp.dot(place[...], feet, preferred_element_type=jnp.float32)
     packed = packed.astype(jnp.bfloat16)
-    rows = sizes.rows
-    end = sizes.lane_tiles * rows
-    for o in range(owners):
-        for n in range(sizes.lane_tiles):
-            send_ref[o, 0, n * rows : (n + 1) * rows, :] = packed[
-                o * rows : (o + 1) * rows, n * LANES : (n + 1) * LANES
-            ]
-        send_ref[o, 0, end : end + 8, :] = first_notes[o].astype(jnp.bfloat16)
+    rows, spill, tiles = sizes.rows, sizes.spill, sizes.lane_tiles
+    end = tiles * rows
+    for c in range(group):
+        for o in range(owners):
+            for n in range(tiles):
+                lanes = slice((c * tiles + n) * LANES, (c * tiles + n + 1) * LANES)
+                send_ref[o, c, n * rows : (n + 1) * rows, :] = packed[
+                    o * rows : (o + 1) * rows, lanes
+                ]
+            send_ref[o, c, end : end + 8, :] = first_notes[o].astype(jnp.bfloat16)
+        for n in range(tiles):
+            lanes = slice((c * tiles + n) * LANES, (c * tiles + n + 1) * LANES)
+            over_rows[c, n * spill : (n + 1) * spill, :] = packed[owners * rows :, lanes]
     for d in range(sizes.columns):
 
-        @pl.when(step == d)
+        @pl.when(step == d // group)
         def _():
-            for n in range(sizes.lane_tiles):
-                spills[d][n * sizes.spill : (n + 1) * sizes.spill, :] = packed[
-                    owners * rows :, n * LANES : (n + 1) * LANES
-                ]
-            end = sizes.lane_tiles * sizes.spill
-            spills[d][end : end + 16, :] = spill_notes[...].astype(jnp.bfloat16)
+            spills[d][: tiles * spill, :] = over_rows[(d ^ at_ref[1]) % group]
+            spills[d][tiles * spill :, :] = spill_notes[...].astype(jnp.bfloat16)
 
 
 def level_of(sizes, ref):
@@ -385,7 +398,6 @@
     owners, columns, devices, part = sizes.owners, sizes.columns, sizes.devices, sizes.part
     both = ("flux", "obs")
     params = pltpu.CompilerParams(vmem_limit_bytes=VMEM_BYTES)
-    smem = pl.BlockSpec(memory_space=pltpu.SMEM)
     me = lax.axis_index("flux") * columns + lax.axis_index("obs")
     at = jnp.stack([me, lax.axis_index("obs"), lax.axis_index("flux")])
     flux = flux.transpose(1, 0, 2)
@@ -393,36 +405,45 @@
     first_height = sizes.lane_tiles * sizes.rows + 8
     spill_height = sizes.lane_tiles * sizes.spill + 16
     all_slots = sizes.slots * sizes.per_slot
+    group = columns // PACK_STEPS
+    tables = (tile_list.T, tile_row, obs_hour.T, observed.T, obs_var.T)
     send, *spills = pl.pallas_call(
         functools.partial(pack_kernel, sizes),
         grid_spec=pltpu.PrefetchScalarGridSpec(
             num_scalar_prefetch=1,
-            grid=(columns,),
-            in_specs=[smem] * 5
-            + [pl.BlockSpec((all_slots, part), lambda d, at: (0, d ^ at[1]))],
+            grid=(PACK_STEPS,),
+            in_specs=[pl.BlockSpec(memory_space=pltpu.HBM)] * 5
+            + [
+                pl.BlockSpec(
+                    (all_slots // sizes.lags, sizes.lags, group * part),
+                    lambda i, at: (0, 0, i ^ (at[1] // group)),
+                )
+            ],
             out_specs=[
-                pl.BlockSpec((owners, 1, first_height, LANES), lambda d, at: (0, d ^ at[1], 0, 0))
+                pl.BlockSpec(
+                    (owners, group, first_height, LANES),
+                    lambda i, at: (0, i ^ (at[1] // group), 0, 0),
+                )
             ]
-            + [pl.BlockSpec((spill_height, LANES), lambda d, at: (0, 0))] * columns,
+            + [pl.BlockSpec((spill_height, LANES), lambda i, at: (0, 0))] * columns,
             scratch_shapes=[
                 pltpu.VMEM((owners * sizes.rows + sizes.spill, all_slots), jnp.bfloat16),
                 pltpu.VMEM((owners, 8, LANES), jnp.float32),
                 pltpu.VMEM((16, LANES), jnp.float32),
+                pltpu.VMEM((group, sizes.lane_tiles * sizes.spill, LANES), jnp.bfloat16),
                 pltpu.SMEM((owners + 1,), jnp.int32),
-            ],
+            ]
+            + [pltpu.SMEM(table.shape, table.dtype) for table in tables]
+            + [pltpu.SemaphoreType.DMA((5,))],
         ),
         out_shape=[pltpu.HBM((owners, columns, first_height, LANES), jnp.bfloat16)]
         + [jax.ShapeDtypeStruct((spill_height, LANES), jnp.bfloat16)] * columns,
-        compiler_params=params,
+        compiler_params=pltpu.CompilerParams(vmem_limit_bytes=ALL_VMEM_BYTES),
         name="pack",
     )(
         at,
-        tile_list.T,
-        tile_row,
-        obs_hour.T,
-        observed.T,
-        obs_var.T,
-        footprint.reshape(all_slots, sizes.lane_tiles * columns * LANES),
+        *tables,
+        footprint.reshape(all_slots // sizes.lags, sizes.lags, columns * part),
     )
     got = lax.all_to_all(
         send.reshape(devices, first_height, LANES), both, split_axis=0, concat_axis=0, tiled=True

time: 112 us -> 108 us (0.964)
  local copies, waits for them, and re-layouts: 3.35 us -> 0.59 us
    reshape x1 -> x0, local copies, waits for them, and re-layouts: 2.77 us -> none  [shards(): footprint.reshape(all_slots, sizes.lane_tiles * columns * LANES)]
where the time goes in v1:
time: 108 us
  waiting for transfers between devices  46 us (43%)
  Pallas kernels  24.7 us (23%)
  starting transfers between devices  18.9 us (17%)
  blocking collectives  16.3 us (15%)
  between operations  1.45 us (1%)
    ppermute x7, waiting for transfers between devices, shards(): lax.ppermute(spills[d], 'obs', [(i, i ^ d) for i in range(columns)])  28.5 us
    all_to_all x1, blocking collectives, run(): sums = lax.all_to_all(sums, both, split_axis=0, concat_axis=0, tiled=True)  16.3 us
    ppermute x3, waiting for transfers between devices, swap(): lax.ppermute(arrays[n], 'flux', [(i, i ^ n) for i in range(owners)])  12.4 us
    all_to_all x1, starting transfers between devices, shards(): lax.all_to_all(send.reshape(devices, first_height, LANES), both, split_ax...  7.31 us
    ppermute x7, starting transfers between devices, shards(): lax.ppermute(spills[d], 'obs', [(i, i ^ d) for i in range(columns)])  6.71 us
    pallas_call x1, Pallas kernels, run(): pl.pallas_call(functools.partial(adjoint_kernel, sizes, chunks), grid_spe...  6.22 us
    pallas_call x1, Pallas kernels, shards(): pl.pallas_call(functools.partial(regroup_kernel, sizes), grid_spec=pltpu....  5.85 us
    pallas_call x1, Pallas kernels, shards(): pl.pallas_call(functools.partial(pack_kernel, sizes), grid_spec=pltpu.Pre...  5.77 us
  transfers between devices with their start and end apart: 11, of which 6 were waited for; matrix products, arithmetic and copies ran while one was open for 0% of the time, Pallas kernels for 9%

profile of v1, /device:TPU:0, one launch (start us, length us, event | category | flops | bytes accessed | tf_op | source)
XLA Modules:
  0.0 107.9 jit_solution(3320025838282511985)
XLA Ops:
  0.6 0.1 pad_add_fusion.at_ref
  0.7 5.8 %pack.1 = (bf16[4,8,264,128]{3,2,1,0:T(8,128)(2,1)}, bf16[528,128]{1,0:T(8,128)(2,1)}, bf16[528,128]{1,0:T(8,128)(2,1)}, bf16[528,128]{1,0:T(8,128)(2,1)}, bf16[...) custom-call(s32[3]{0:T(128)S(1)} %pad_add_fusion.at_ref, ...), custom_call_target="tpu_custom_call" | custom-call | tf_op jit(solution)/shard_map/pack/pallas_call | solution.py:410
  6.5 0.0 copy-start.11
  6.5 0.0 copy-start.10
  6.5 0.0 copy-start.9
  6.5 0.0 copy-start.8
  6.5 0.0 copy-start.7
  6.5 0.0 copy-start.6
  6.5 0.0 copy-start.5
  6.6 0.0 copy-start
  6.6 7.3 %all-to-all-start.3 = ((bf16[32,264,128]{2,1,0:T(8,128)(2,1)}), bf16[32,264,128]{2,1,0:T(8,128)(2,1)S(1)}, u32[]{:S(2)}, u32[]{:S(2)}) async-start(bf16[32,264,128]{2,1,0:T(8,128)(2,1)} %bitcast.19), calls=%async_computation.3 | async-start | bytes 4325376 | tf_op jit(solution)/shard_map/all_to_all | solution.py:448
  13.9 0.0 copy-done.11
  13.9 0.3 collective-permute-start.6
  14.2 0.0 copy-done.10
  14.2 1.7 %collective-permute-start.7 = (bf16[528,128]{1,0:T(8,128)(2,1)S(1)}, bf16[528,128]{1,0:T(8,128)(2,1)S(1)}, u32[]{:S(2)}, u32[]{:S(2)}) collective-permute-start(bf16[528,128]{1,0:T(8,128)(2,1)S(1)} %copy-done.10), channel_id=1, source_target_pairs={{0,2},{1,3},{2,0},{3,1},{4,6},{5,7},{6,4},{7,5},{8,10},{9,11},{10,... | collective-permute-start | bytes 405512 | tf_op jit(solution)/shard_map/ppermute | solution.py:452
  15.9 0.0 copy-done.9
  15.9 0.0 collective-permute-start.8
  15.9 0.0 copy-done.8
  15.9 1.7 %collective-permute-start.9 = (bf16[528,128]{1,0:T(8,128)(2,1)S(1)}, bf16[528,128]{1,0:T(8,128)(2,1)S(1)}, u32[]{:S(2)}, u32[]{:S(2)}) collective-permute-start(bf16[528,128]{1,0:T(8,128)(2,1)S(1)} %copy-done.8), channel_id=1, source_target_pairs={{0,4},{1,5},{2,6},{3,7},{4,0},{5,1},{6,2},{7,3},{8,12},{9,13},{10,... | collective-permute-start | bytes 405512 | tf_op jit(solution)/shard_map/ppermute | solution.py:452
  17.6 0.0 copy-done.7
  17.6 0.1 collective-permute-start.10
  17.7 0.0 collective-permute-done.6.refs_1_
  17.7 0.0 copy-done.6
  17.7 2.6 %collective-permute-start.11 = (bf16[528,128]{1,0:T(8,128)(2,1)S(1)}, bf16[528,128]{1,0:T(8,128)(2,1)S(1)}, u32[]{:S(2)}, u32[]{:S(2)}) collective-permute-start(bf16[528,128]{1,0:T(8,128)(2,1)S(1)} %copy-done.6), channel_id=1, source_target_pairs={{0,6},{1,7},{2,4},{3,5},{4,2},{5,3},{6,0},{7,1},{8,14},{9,15},{10,... | collective-permute-start | bytes 405512 | tf_op jit(solution)/shard_map/ppermute | solution.py:452
  20.3 13.5 %collective-permute-done.7.refs_2_ = bf16[528,128]{1,0:T(8,128)(2,1)S(1)} collective-permute-done((bf16[528,128]{1,0:T(8,128)(2,1)S(1)}, bf16[528,128]{1,0:T(8,128)(2,1)S(1)}, u32[]{:S(2)}, u32[]{:S(2)}) %collective-permute-start.7) | collective-permute-done | bytes 135200 | tf_op jit(solution)/shard_map/ppermute | solution.py:452
  33.8 0.0 copy-done.5
  33.8 0.3 collective-permute-start.12
  34.1 4.5 %collective-permute-done.8.refs_3_ = bf16[528,128]{1,0:T(8,128)(2,1)S(1)} collective-permute-done((bf16[528,128]{1,0:T(8,128)(2,1)S(1)}, bf16[528,128]{1,0:T(8,128)(2,1)S(1)}, u32[]{:S(2)}, u32[]{:S(2)}) %collective-permute-start.8) | collective-permute-done | bytes 135200 | tf_op jit(solution)/shard_map/ppermute | solution.py:452
  38.6 0.0 collective-permute-done.9.refs_4_
  38.6 0.0 collective-permute-done.10.refs_5_
  38.6 8.3 %collective-permute-done.11.refs_6_ = bf16[528,128]{1,0:T(8,128)(2,1)S(1)} collective-permute-done((bf16[528,128]{1,0:T(8,128)(2,1)S(1)}, bf16[528,128]{1,0:T(8,128)(2,1)S(1)}, u32[]{:S(2)}, u32[]{:S(2)}) %collective-permute-start.11) | collective-permute-done | bytes 135200 | tf_op jit(solution)/shard_map/ppermute | solution.py:452
  46.9 2.2 %collective-permute-done.12.refs_7_ = bf16[528,128]{1,0:T(8,128)(2,1)S(1)} collective-permute-done((bf16[528,128]{1,0:T(8,128)(2,1)S(1)}, bf16[528,128]{1,0:T(8,128)(2,1)S(1)}, u32[]{:S(2)}, u32[]{:S(2)}) %collective-permute-start.12) | collective-permute-done | bytes 135200 | tf_op jit(solution)/shard_map/ppermute | solution.py:452
  49.1 0.0 copy-done
  49.1 5.8 %regroup.1 = (bf16[264,512]{1,0:T(8,128)(2,1)S(1)}, bf16[264,512]{1,0:T(8,128)(2,1)S(1)}, bf16[264,512]{1,0:T(8,128)(2,1)S(1)}, bf16[264,512]{1,0:T(8,128)(2,1)S...) custom-call(s32[3]{0:T(128)S(1)} %pad_add_fusion.at_ref, ...), custom_call_target="tpu_custom_call" | custom-call | tf_op jit(solution)/shard_map/regroup/pallas_call | solution.py:458
  55.0 0.6 collective-permute-start.13
  55.6 4.2 %collective-permute-start.14 = (bf16[264,512]{1,0:T(8,128)(2,1)S(1)}, bf16[264,512]{1,0:T(8,128)(2,1)}, u32[]{:S(2)}, u32[]{:S(2)}) collective-permute-start(bf16[264,512]{1,0:T(8,128)(2,1)S(1)} %get-tuple-element.129), channel_id=1, source_target_pairs={{0,16},{8,24},{16,0},{24,8},{1,17},{9,25},{17,1},{25,9},{2,18},{10... | collective-permute-start | bytes 811016 | tf_op jit(solution)/shard_map/ppermute | solution.py:478
  59.8 0.0 collective-permute-start.15
  59.8 5.1 %all-to-all-done.3.got_ref.all_ref = bf16[32,264,128]{2,1,0:T(8,128)(2,1)S(1)} async-done(((bf16[32,264,128]{2,1,0:T(8,128)(2,1)}), bf16[32,264,128]{2,1,0:T(8,128)(2,1)S(1)}, u32[]{:S(2)}, u32[]{:S(2)}) %all-to-all-start.3) | async-done | bytes 2162720 | tf_op jit(solution)/shard_map/all_to_all | solution.py:448
  64.9 3.9 %forward_first.1 = (f32[8,128]{1,0:T(8,128)S(1)}, s32[8,128]{1,0:T(8,128)S(1)}) custom-call(s32[3]{0:T(128)S(1)} %pad_add_fusion.at_ref, bf16[5,128,4096]{2,1,0:T(8,128)(2,1)} %bitcast.15, bf16[32,264,128]{2,1,0:T(8,128)(2,1)S(1)} %all-to-all-done.3.got_ref.all_ref, bf16[32,264,128]{2,1,0:T(8,128)(2,1)S(1)} %all-to-all-done.3.got_ref.all_ref), custom_call_target="tpu_custom_call" | custom-call | tf_op jit(solution)/shard_map/forward_first/pallas_call | solution.py:491
  68.8 0.5 slice.12
  70.0 0.0 collective-permute-done.13.refs_1_
  70.0 12.4 %collective-permute-done.14.refs_2_ = bf16[264,512]{1,0:T(8,128)(2,1)} collective-permute-done((bf16[264,512]{1,0:T(8,128)(2,1)S(1)}, bf16[264,512]{1,0:T(8,128)(2,1)}, u32[]{:S(2)}, u32[]{:S(2)}) %collective-permute-start.14) | collective-permute-done | bytes 270368 | tf_op jit(solution)/shard_map/ppermute | solution.py:478
  82.4 0.0 collective-permute-done.15.refs_3_
  82.4 0.0 copy-start.1
  82.4 0.0 copy-start.2
  82.4 0.0 copy-start.3
  82.4 0.0 copy-start.4
  82.4 3.0 %forward_second.1 = f32[32,8,128]{2,1,0:T(8,128)S(1)} custom-call(s32[3]{0:T(128)S(1)} %pad_add_fusion.at_ref, bf16[5,128,4096]{2,1,0:T(8,128)(2,1)} %bitcast.16, f32[1,8,128]{2,1,0:T(8,128)S(1)} %bitcast.14, bf16[264,512]{1,0:T(8,128)(2,1)S(1)} %get-tuple-element.127.refs_0_, bf16[264,512]{1,0:T(8,128)(2,1)} %collective-permute-done.13.refs_1_, ...), custom_call_target="tpu_custom_call" | custom-call | tf_op jit(solution)/shard_map/forward_second/pallas_call | solution.py:515
  85.3 0.0 copy-done.1
  85.4 0.0 copy-done.2
  85.4 0.0 copy-done.3
  85.4 0.0 copy-done.4
  85.4 22.5 %conditional.1 = ((f32[4,8]{1,0:T(4,128)}, f32[5,128,512]{2,1,0:T(8,128)})) conditional(s32[]{:T(128)} %bitcast.10, (f32[32,8,128]{2,1,0:T(8,128)S(1)}, s32[3]{0:T(128)S(1)}, bf16[32,264,128]{2,1,0:T(8,128)(2,1)S(1)}, bf16[264,512]{1,0:T(8,128)(2,1)S(1)}, bf16[264,512]{1,0:T(8,128)(2,1)}, /*index=5*/bf16[264,512]{1,0:T(8,128)(2,1)}, ...), branch_computations={%region_0.0_spmd, %region_1.0_spmd, %region_2.0_spmd} | conditional | bytes 3408000 | solution.py:575
  85.4 16.3 %all_to_all.17.sums_ref = f32[32,8,128]{2,1,0:T(8,128)S(1)} all-to-all(f32[32,8,128]{2,1,0:T(8,128)S(1)} %get-tuple-element.63), channel_id=1, replica_groups=mesh['flux'=4,'obs'=8] {'flux','obs'}, dimensions={0} | all-to-all | bytes 262144 | tf_op jit(solution)/shard_map/cond/branch_0_fun/all_to_all | solution.py:542
  101.7 6.2 %adjoint.3 = (f32[4,8]{1,0:T(4,128)}, f32[5,128,512]{2,1,0:T(8,128)}) custom-call(s32[3]{0:T(128)S(1)} %get-tuple-element.62.at_ref, f32[32,8,128]{2,1,0:T(8,128)S(1)} %all_to_all.17.sums_ref, bf16[32,264,128]{2,1,0:T(8,128)(2,1)S(1)} %get-tuple-element.64.one_ref, bf16[264,512]{1,0:T(8,128)(2,1)S(1)} %get-tuple-element.65.refs_0_, ...), custom_call_target="tpu_custom_call" | custom-call | tf_op jit(solution)/shard_map/cond/branch_0_fun/adjoint/pallas_call | solution.py:545
Async XLA Ops:
  6.5 7.4 %copy-start.11 = (bf16[528,128]{1,0:T(8,128)(2,1)S(1)}, bf16[528,128]{1,0:T(8,128)(2,1)}, u32[]{:S(2)}) copy-start(bf16[528,128]{1,0:T(8,128)(2,1)} %get-tuple-element.120) | copy-start | bytes 405508
  6.5 7.7 %copy-start.10 = (bf16[528,128]{1,0:T(8,128)(2,1)S(1)}, bf16[528,128]{1,0:T(8,128)(2,1)}, u32[]{:S(2)}) copy-start(bf16[528,128]{1,0:T(8,128)(2,1)} %get-tuple-element.121) | copy-start | bytes 405508
  6.5 9.4 %copy-start.9 = (bf16[528,128]{1,0:T(8,128)(2,1)S(1)}, bf16[528,128]{1,0:T(8,128)(2,1)}, u32[]{:S(2)}) copy-start(bf16[528,128]{1,0:T(8,128)(2,1)} %get-tuple-element.122) | copy-start | bytes 405508
  6.5 9.4 %copy-start.8 = (bf16[528,128]{1,0:T(8,128)(2,1)S(1)}, bf16[528,128]{1,0:T(8,128)(2,1)}, u32[]{:S(2)}) copy-start(bf16[528,128]{1,0:T(8,128)(2,1)} %get-tuple-element.123) | copy-start | bytes 405508
  6.5 11.1 %copy-start.7 = (bf16[528,128]{1,0:T(8,128)(2,1)S(1)}, bf16[528,128]{1,0:T(8,128)(2,1)}, u32[]{:S(2)}) copy-start(bf16[528,128]{1,0:T(8,128)(2,1)} %get-tuple-element.124) | copy-start | bytes 405508
  6.5 11.2 %copy-start.6 = (bf16[528,128]{1,0:T(8,128)(2,1)S(1)}, bf16[528,128]{1,0:T(8,128)(2,1)}, u32[]{:S(2)}) copy-start(bf16[528,128]{1,0:T(8,128)(2,1)} %get-tuple-element.125) | copy-start | bytes 405508
  6.5 27.2 %copy-start.5 = (bf16[528,128]{1,0:T(8,128)(2,1)S(1)}, bf16[528,128]{1,0:T(8,128)(2,1)}, u32[]{:S(2)}) copy-start(bf16[528,128]{1,0:T(8,128)(2,1)} %get-tuple-element.126) | copy-start | bytes 405508
  6.6 42.6 %copy-start = (bf16[528,128]{1,0:T(8,128)(2,1)S(1)}, bf16[528,128]{1,0:T(8,128)(2,1)}, u32[]{:S(2)}) copy-start(bf16[528,128]{1,0:T(8,128)(2,1)} %get-tuple-element.119.refs_0_) | copy-start | bytes 405508
  6.6 58.4 %all-to-all-start.3 = ((bf16[32,264,128]{2,1,0:T(8,128)(2,1)}), bf16[32,264,128]{2,1,0:T(8,128)(2,1)S(1)}, u32[]{:S(2)}, u32[]{:S(2)}) async-start(bf16[32,264,128]{2,1,0:T(8,128)(2,1)} %bitcast.19), calls=%async_computation.3 | async-start | bytes 4325376 | tf_op jit(solution)/shard_map/all_to_all | solution.py:448
  13.9 3.8 %collective-permute-start.6 = (bf16[528,128]{1,0:T(8,128)(2,1)S(1)}, bf16[528,128]{1,0:T(8,128)(2,1)S(1)}, u32[]{:S(2)}, u32[]{:S(2)}) collective-permute-start(bf16[528,128]{1,0:T(8,128)(2,1)S(1)} %copy-done.11), channel_id=1, source_target_pairs={{0,1},{1,0},{2,3},{3,2},{4,5},{5,4},{6,7},{7,6},{8,9},{9,8},{10,11... | collective-permute-start | bytes 405512 | tf_op jit(solution)/shard_map/ppermute | solution.py:452
  14.2 19.6 %collective-permute-start.7 = (bf16[528,128]{1,0:T(8,128)(2,1)S(1)}, bf16[528,128]{1,0:T(8,128)(2,1)S(1)}, u32[]{:S(2)}, u32[]{:S(2)}) collective-permute-start(bf16[528,128]{1,0:T(8,128)(2,1)S(1)} %copy-done.10), channel_id=1, source_target_pairs={{0,2},{1,3},{2,0},{3,1},{4,6},{5,7},{6,4},{7,5},{8,10},{9,11},{10,... | collective-permute-start | bytes 405512 | tf_op jit(solution)/shard_map/ppermute | solution.py:452
  15.9 22.7 %collective-permute-start.8 = (bf16[528,128]{1,0:T(8,128)(2,1)S(1)}, bf16[528,128]{1,0:T(8,128)(2,1)S(1)}, u32[]{:S(2)}, u32[]{:S(2)}) collective-permute-start(bf16[528,128]{1,0:T(8,128)(2,1)S(1)} %copy-done.9), channel_id=1, source_target_pairs={{0,3},{1,2},{2,1},{3,0},{4,7},{5,6},{6,5},{7,4},{8,11},{9,10},{10,... | collective-permute-start | bytes 405512 | tf_op jit(solution)/shard_map/ppermute | solution.py:452
  15.9 22.7 %collective-permute-start.9 = (bf16[528,128]{1,0:T(8,128)(2,1)S(1)}, bf16[528,128]{1,0:T(8,128)(2,1)S(1)}, u32[]{:S(2)}, u32[]{:S(2)}) collective-permute-start(bf16[528,128]{1,0:T(8,128)(2,1)S(1)} %copy-done.8), channel_id=1, source_target_pairs={{0,4},{1,5},{2,6},{3,7},{4,0},{5,1},{6,2},{7,3},{8,12},{9,13},{10,... | collective-permute-start | bytes 405512 | tf_op jit(solution)/shard_map/ppermute | solution.py:452
  17.6 21.0 %collective-permute-start.10 = (bf16[528,128]{1,0:T(8,128)(2,1)S(1)}, bf16[528,128]{1,0:T(8,128)(2,1)S(1)}, u32[]{:S(2)}, u32[]{:S(2)}) collective-permute-start(bf16[528,128]{1,0:T(8,128)(2,1)S(1)} %copy-done.7), channel_id=1, source_target_pairs={{0,5},{1,4},{2,7},{3,6},{4,1},{5,0},{6,3},{7,2},{8,13},{9,12},{10,... | collective-permute-start | bytes 405512 | tf_op jit(solution)/shard_map/ppermute | solution.py:452
  17.7 29.2 %collective-permute-start.11 = (bf16[528,128]{1,0:T(8,128)(2,1)S(1)}, bf16[528,128]{1,0:T(8,128)(2,1)S(1)}, u32[]{:S(2)}, u32[]{:S(2)}) collective-permute-start(bf16[528,128]{1,0:T(8,128)(2,1)S(1)} %copy-done.6), channel_id=1, source_target_pairs={{0,6},{1,7},{2,4},{3,5},{4,2},{5,3},{6,0},{7,1},{8,14},{9,15},{10,... | collective-permute-start | bytes 405512 | tf_op jit(solution)/shard_map/ppermute | solution.py:452
  33.8 15.3 %collective-permute-start.12 = (bf16[528,128]{1,0:T(8,128)(2,1)S(1)}, bf16[528,128]{1,0:T(8,128)(2,1)S(1)}, u32[]{:S(2)}, u32[]{:S(2)}) collective-permute-start(bf16[528,128]{1,0:T(8,128)(2,1)S(1)} %copy-done.5), channel_id=1, source_target_pairs={{0,7},{1,6},{2,5},{3,4},{4,3},{5,2},{6,1},{7,0},{8,15},{9,14},{10,... | collective-permute-start | bytes 405512 | tf_op jit(solution)/shard_map/ppermute | solution.py:452
  55.0 15.0 %collective-permute-start.13 = (bf16[264,512]{1,0:T(8,128)(2,1)S(1)}, bf16[264,512]{1,0:T(8,128)(2,1)}, u32[]{:S(2)}, u32[]{:S(2)}) collective-permute-start(bf16[264,512]{1,0:T(8,128)(2,1)S(1)} %get-tuple-element.128), channel_id=1, source_target_pairs={{0,8},{8,0},{16,24},{24,16},{1,9},{9,1},{17,25},{25,17},{2,10},{10... | collective-permute-start | bytes 811016 | tf_op jit(solution)/shard_map/ppermute | solution.py:478
  55.6 26.8 %collective-permute-start.14 = (bf16[264,512]{1,0:T(8,128)(2,1)S(1)}, bf16[264,512]{1,0:T(8,128)(2,1)}, u32[]{:S(2)}, u32[]{:S(2)}) collective-permute-start(bf16[264,512]{1,0:T(8,128)(2,1)S(1)} %get-tuple-element.129), channel_id=1, source_target_pairs={{0,16},{8,24},{16,0},{24,8},{1,17},{9,25},{17,1},{25,9},{2,18},{10... | collective-permute-start | bytes 811016 | tf_op jit(solution)/shard_map/ppermute | solution.py:478
  59.8 22.5 %collective-permute-start.15 = (bf16[264,512]{1,0:T(8,128)(2,1)S(1)}, bf16[264,512]{1,0:T(8,128)(2,1)}, u32[]{:S(2)}, u32[]{:S(2)}) collective-permute-start(bf16[264,512]{1,0:T(8,128)(2,1)S(1)} %get-tuple-element.130), channel_id=1, source_target_pairs={{0,24},{8,16},{16,8},{24,0},{1,25},{9,17},{17,9},{25,1},{2,26},{10... | collective-permute-start | bytes 811016 | tf_op jit(solution)/shard_map/ppermute | solution.py:478
  82.4 3.0 %copy-start.1 = (bf16[256,512]{1,0:T(8,128)(2,1)S(1)}, bf16[256,512]{1,0:T(8,128)(2,1)}, u32[]{:S(2)}) copy-start(bf16[256,512]{1,0:T(8,128)(2,1)} %get-tuple-element.134) | copy-start | bytes 786436
  82.4 3.0 %copy-start.2 = (bf16[256,512]{1,0:T(8,128)(2,1)S(1)}, bf16[256,512]{1,0:T(8,128)(2,1)}, u32[]{:S(2)}) copy-start(bf16[256,512]{1,0:T(8,128)(2,1)} %get-tuple-element.131) | copy-start | bytes 786436
  82.4 3.0 %copy-start.3 = (bf16[256,512]{1,0:T(8,128)(2,1)S(1)}, bf16[256,512]{1,0:T(8,128)(2,1)}, u32[]{:S(2)}) copy-start(bf16[256,512]{1,0:T(8,128)(2,1)} %get-tuple-element.132) | copy-start | bytes 786436
  82.4 3.0 %copy-start.4 = (bf16[256,512]{1,0:T(8,128)(2,1)S(1)}, bf16[256,512]{1,0:T(8,128)(2,1)}, u32[]{:S(2)}) copy-start(bf16[256,512]{1,0:T(8,128)(2,1)} %get-tuple-element.133) | copy-start | bytes 786436

commit v2 on v1

v2 whole, which is shorter than its diff:
```python
import functools

import jax
import jax.numpy as jnp
from jax import lax
from jax.experimental import pallas as pl
from jax.experimental.pallas import tpu as pltpu
from jax.sharding import PartitionSpec as P

LANES = 128
VMEM_BYTES = 48 * 1024 * 1024
ALL_VMEM_BYTES = 60 * 1024 * 1024
BASE = 8
REST = (0, 2, 8)
PACK_STEPS = 2


def iota(shape, dim):
    return lax.broadcasted_iota(jnp.int32, shape, dim)


def thirds(value):
    high = value.astype(jnp.bfloat16).astype(jnp.float32)
    rest = value - high
    middle = rest.astype(jnp.bfloat16).astype(jnp.float32)
    return high, middle, (rest - middle).astype(jnp.bfloat16).astype(jnp.float32)


class Sizes:
    def __init__(self, owners, columns, footprint, flux):
        self.owners, self.columns = owners, columns
        self.devices = owners * columns
        self.blocks, self.width, self.soundings, self.lags, cells = footprint
        self.tiles, self.hours = flux[0], flux[1]
        self.span = self.hours - self.lags + 1
        self.half = self.span * self.tiles // 2
        self.slots = self.blocks * self.width
        self.per_slot = self.soundings * self.lags
        self.part = cells // columns
        self.lane_tiles = self.part // LANES
        self.first = self.slots // owners
        self.rows = self.first * self.per_slot
        self.spill = self.slots // 2 * self.per_slot
        self.second = columns * self.first * self.per_slot
        self.base = self.second * BASE // 16
        self.notes = 8 * (self.second // self.part)
        self.states = self.blocks * self.soundings
        self.per_page = 8 * LANES // self.states
        self.pages = self.devices // self.per_page


def read_notes(sizes, notes, plane):
    lane = iota((1, notes.shape[1]), 1)
    inner = lax.rem(lane, jnp.int32(sizes.per_slot))
    base = notes[0:1]
    target = (base + sizes.half).astype(jnp.int32) + lax.rem(inner, jnp.int32(sizes.lags)) * sizes.tiles
    target = jnp.where(base > sizes.half - 0.5, -1, target)
    place = notes[1:2].astype(jnp.int32)
    block = lax.rem(place, jnp.int32(sizes.blocks))
    device = plane * sizes.columns + lax.div(place, jnp.int32(sizes.blocks))
    state = block * sizes.soundings + lax.div(inner, jnp.int32(sizes.lags))
    row = lax.div(device, jnp.int32(sizes.per_page)) * 8 + lax.rem(state, jnp.int32(8))
    column = lax.div(state, jnp.int32(8)) * sizes.per_page + lax.rem(device, jnp.int32(sizes.per_page))
    seen = notes[2:3] + notes[3:4] + notes[4:5]
    spread = notes[5:6] + notes[6:7] + notes[7:8]
    places = [each.astype(jnp.float32) for each in (target, row, column)]
    return jnp.concatenate(places + [seen, spread, jnp.zeros((3, lane.shape[1]), jnp.float32)], axis=0)


def first_round(sizes, ref, step):
    sources, count = ref.shape[0], sizes.rows
    feet = jnp.concatenate(
        [
            ref[:, n * count : (n + 1) * count, :].reshape(sources * count, LANES)
            for n in range(sizes.lane_tiles)
        ],
        axis=1,
    )
    end = sizes.lane_tiles * count
    notes = jnp.concatenate(
        [ref[s, end : end + 8, :].astype(jnp.float32)[:, :count] for s in range(sources)], axis=1
    )
    lane = iota((1, sources * count), 1)
    plane = lax.div(step * sources + lax.div(lane, jnp.int32(count)), jnp.int32(sizes.columns))
    return feet, notes, plane


def second_round(sizes, flux_index, bases, rests, with_bases=True):
    notes = [
        jnp.concatenate(
            [ref[n * 8 : (n + 1) * 8, :].astype(jnp.float32) for n in range(sizes.notes // 8)],
            axis=1,
        )
        for ref in bases
    ]
    feet, kept, planes = [], [], []
    if with_bases:
        feet += [ref[sizes.notes :, :] for ref in bases]
        kept += [each[:, : sizes.base] for each in notes]
        planes.append(lax.div(iota((1, len(bases) * sizes.base), 1), jnp.int32(sizes.base)))
    if rests:
        more = rests[0].shape[0]
        feet += [ref[...] for ref in rests]
        kept += [each[:, sizes.base : sizes.base + more] for each in notes]
        planes.append(lax.div(iota((1, len(rests) * more), 1), jnp.int32(more)))
    plane = lax.bitwise_xor(jnp.concatenate(planes, axis=1), flux_index)
    return jnp.concatenate(feet, axis=0), jnp.concatenate(kept, axis=1), plane


def partial_sums(sizes, flux_ref, feet, read):
    target, row, column = (read[n : n + 1].astype(jnp.int32) for n in range(3))
    count = feet.shape[0]
    levels = sizes.hours * sizes.tiles
    products = lax.dot_general(
        flux_ref[...].reshape(levels, sizes.part),
        feet,
        (((1,), (1,)), ((), ())),
        preferred_element_type=jnp.float32,
    )
    chosen = jnp.where(iota((levels, count), 0) == target, products, 0.0)
    partial = jnp.sum(chosen, axis=0, keepdims=True)
    height = 8 * sizes.pages
    spread = jnp.where(iota((height, count), 0) == row, partial, 0.0)
    terms = jnp.concatenate(thirds(spread), axis=0).astype(jnp.bfloat16)
    lanes = (iota((LANES, count), 0) == column).astype(jnp.bfloat16)
    sums = lax.dot_general(
        terms, lanes, (((1,), (1,)), ((), ())), preferred_element_type=jnp.float32
    )
    return sums[:height] + sums[height : 2 * height] + sums[2 * height :]


def coefficients(sizes, model, read):
    target, row, column = (read[n : n + 1].astype(jnp.int32) for n in range(3))
    count = read.shape[1]
    height = 8 * sizes.pages
    lanes = (iota((LANES, count), 0) == column).astype(jnp.bfloat16)
    taken = jnp.dot(model, lanes, preferred_element_type=jnp.float32)
    taken = taken[:height] + taken[height : 2 * height] + taken[2 * height :]
    value = jnp.sum(
        jnp.where(iota((height, count), 0) == row, taken, 0.0), axis=0, keepdims=True
    )
    scaled = ((value - read[3:4]) / read[4:5]).astype(jnp.bfloat16).astype(jnp.float32)
    levels = sizes.hours * sizes.tiles
    return jnp.where(iota((levels, count), 0) == target, scaled, 0.0).astype(jnp.bfloat16)


def pack_kernel(sizes, at_ref, *refs):
    tables, feet_ref, send_ref = refs[:5], refs[5], refs[6]
    spills = refs[7 : 7 + sizes.columns]
    feet, sent, spilled, first_notes, count, *local = refs[7 + sizes.columns : -4]
    arrived, feet_arrived, sent_done, over_done = refs[-4:]
    list_ref, row_ref, hour_ref, seen_ref, var_ref = local
    owners, per_slot = sizes.owners, sizes.per_slot
    group = sizes.columns // PACK_STEPS
    mine = at_ref[1]
    tables = [
        pltpu.make_async_copy(table, here, arrived.at[n])
        for n, (table, here) in enumerate(zip(tables, local))
    ]
    for copy in tables:
        copy.start()
    firsts = [pl.multiple_of((i ^ (mine // group)) * group, group) for i in range(PACK_STEPS)]
    loads = []
    for i, first in enumerate(firsts):
        lanes = pl.ds(pl.multiple_of(first * sizes.part, LANES), group * sizes.part)
        loads.append(
            pltpu.make_async_copy(feet_ref.at[:, :, lanes], feet.at[i], feet_arrived.at[i])
        )
        loads[-1].start()
    for copy in tables:
        copy.wait()

    field, lane = iota((16, LANES), 0), iota((16, LANES), 1)
    inner = lane % per_slot
    sounding = inner // sizes.lags
    slot_at = lane // per_slot
    key_at = iota((1, sizes.slots * per_slot), 1)
    key = jnp.zeros(key_at.shape, jnp.int32)
    empty = jnp.where(field == 0, jnp.float32(sizes.half), 0.0)
    empty = jnp.where(field == 5, 1.0, jnp.where(field == 8, -1.0, empty))
    for o in range(owners):
        count[o] = 0
        first_notes[o] = empty[:8]
    count[owners] = 0
    left = empty
    for b in range(sizes.blocks):
        base = jnp.zeros(field.shape, jnp.float32)
        seen = jnp.zeros(field.shape, jnp.float32)
        spread = jnp.ones(field.shape, jnp.float32)
        for o in range(sizes.soundings):
            here = sounding == o
            hour = hour_ref[o, b] * sizes.tiles - sizes.half
            base = jnp.where(here, hour.astype(jnp.float32), base)
            seen = jnp.where(here, seen_ref[o, b], seen)
            spread = jnp.where(here, var_ref[o, b], spread)
        column = (b + sizes.blocks * at_ref[1]).astype(jnp.float32)
        pattern = jnp.where(field == 0, base, jnp.where(field == 1, column, 0.0))
        for n, term in enumerate(thirds(seen) + thirds(spread)):
            pattern = jnp.where(field == 2 + n, term, pattern)
        for k in range(sizes.width):
            stored = row_ref[list_ref[k, b]]
            owner = lax.div(stored, jnp.int32(sizes.tiles))
            tile = (stored - owner * sizes.tiles).astype(jnp.float32)
            position = count[owner]
            count[owner] = position + 1
            keep = position < sizes.first
            over = count[owners]
            count[owners] = over + jnp.where(keep, 0, 1)
            goes = jnp.where(
                keep, owner * sizes.first + position, owners * sizes.first + over
            )
            value = jnp.where(field == 0, pattern + tile, pattern)
            value = jnp.where(field == 8, owner.astype(jnp.float32), value)
            value = jnp.where(
                field == 9, (position - sizes.first).astype(jnp.float32), value
            )
            first_notes[owner] = jnp.where(
                slot_at[:8] == jnp.where(keep, position, -1), value[:8], first_notes[owner]
            )
            left = jnp.where(slot_at == jnp.where(keep, -1, over), value, left)
            key = jnp.where(
                key_at // per_slot == b * sizes.width + k,
                goes * per_slot + key_at % per_slot,
                key,
            )
    counts = jnp.zeros((8, LANES), jnp.float32)
    for o in range(owners):
        over = jnp.maximum(count[o] - sizes.first, 0).astype(jnp.float32)
        counts = jnp.where(lane[:8] == sizes.rows + o, over, counts)
    for o in range(owners):
        first_notes[o] = jnp.where(lane[:8] < sizes.rows, first_notes[o], counts)
    place = (iota((owners * sizes.rows + sizes.spill, key.shape[1]), 0) == key).astype(
        jnp.bfloat16
    )
    rows, spill, tiles = sizes.rows, sizes.spill, sizes.lane_tiles
    end = tiles * rows
    stores = []
    for i, first in enumerate(firsts):
        loads[i].wait()
        packed = jnp.dot(
            place,
            feet[i].reshape(key.shape[1], group * sizes.part),
            preferred_element_type=jnp.float32,
        ).astype(jnp.bfloat16)
        for c in range(group):
            for o in range(owners):
                for n in range(tiles):
                    lanes = slice((c * tiles + n) * LANES, (c * tiles + n + 1) * LANES)
                    sent[i, o, c, n * rows : (n + 1) * rows, :] = packed[
                        o * rows : (o + 1) * rows, lanes
                    ]
                sent[i, o, c, end : end + 8, :] = first_notes[o].astype(jnp.bfloat16)
            for n in range(tiles):
                lanes = slice((c * tiles + n) * LANES, (c * tiles + n + 1) * LANES)
                spilled[i, c, n * spill : (n + 1) * spill, :] = packed[owners * rows :, lanes]
            spilled[i, c, tiles * spill :, :] = left.astype(jnp.bfloat16)
        stores.append(
            pltpu.make_async_copy(
                sent.at[i], send_ref.at[:, pl.ds(first, group)], sent_done.at[i]
            )
        )
        stores[-1].start()
        for d in range(i * group, (i + 1) * group):
            stores.append(
                pltpu.make_async_copy(spilled.at[i, (d ^ mine) % group], spills[d], over_done.at[d])
            )
            stores[-1].start()
    for copy in stores:
        copy.wait()


def level_of(sizes, ref):
    planes = [
        sum(
            ref[p * sizes.columns + j].astype(jnp.float32) for j in range(sizes.columns)
        )
        for p in range(sizes.owners)
    ]
    counts = functools.reduce(jnp.maximum, planes)[0:1]
    lane = iota(counts.shape, 1)
    counts = jnp.where((lane >= sizes.rows) & (lane < sizes.rows + sizes.owners), counts, 0.0)
    most = jnp.max(counts, axis=1, keepdims=True) * sizes.per_slot
    level = jnp.zeros((1, 1), jnp.int32)
    for n in REST[:-1]:
        level = level + jnp.where(most > sizes.base + sizes.second * n // 16, 1, 0)
    return level


def regroup_kernel(sizes, at_ref, *refs):
    columns, owners, spill = sizes.columns, sizes.owners, sizes.spill
    spills, bases = refs[:columns], refs[columns : columns + owners]
    rests = refs[columns + owners : columns + 2 * owners]
    feet, notes, place = refs[columns + 2 * owners :]
    step = pl.program_id(0)
    owner = at_ref[2] ^ step
    end = sizes.lane_tiles * spill

    @pl.when(step == 0)
    def _():
        for d, ref in enumerate(spills):
            for n in range(sizes.lane_tiles):
                feet[d * spill : (d + 1) * spill, n * LANES : (n + 1) * LANES] = ref[
                    n * spill : (n + 1) * spill, :
                ]
            notes[:, d * spill : (d + 1) * spill] = ref[end : end + 16, :].astype(jnp.float32)

    mine = notes[8:9, :] == owner.astype(jnp.float32)
    total = jnp.zeros((1, 1), jnp.float32)
    keys = []
    for d in range(columns):
        here = mine[:, d * spill : (d + 1) * spill]
        position = total + notes[9:10, d * spill : (d + 1) * spill]
        inner = lax.rem(iota((1, spill), 1), jnp.int32(sizes.per_slot))
        keys.append(
            jnp.where(here, position.astype(jnp.int32) * sizes.per_slot + inner, -1)
        )
        total = total + jnp.sum(
            jnp.where(here, 1.0 / sizes.per_slot, 0.0), axis=1, keepdims=True
        )
    key = jnp.concatenate(keys, axis=1)
    place[...] = (iota(place.shape, 0) == key).astype(jnp.bfloat16)
    sorted_feet = jnp.dot(place[...], feet[...], preferred_element_type=jnp.float32)
    sorted_feet = sorted_feet.astype(jnp.bfloat16)
    moved = lax.dot_general(
        notes[0:8, :].astype(jnp.bfloat16),
        place[...],
        (((1,), (1,)), ((), ())),
        preferred_element_type=jnp.float32,
    )
    field, lane = iota(moved.shape, 0), iota(moved.shape, 1)
    empty = jnp.where(field == 0, jnp.float32(sizes.half), jnp.where(field == 5, 1.0, 0.0))
    moved = jnp.where(lane.astype(jnp.float32) < total * sizes.per_slot, moved, empty)
    moved = moved.astype(jnp.bfloat16)
    for o in range(owners):

        @pl.when(step == o)
        def _():
            for n in range(sizes.notes // 8):
                bases[o][n * 8 : (n + 1) * 8, :] = moved[
                    :, n * sizes.part : (n + 1) * sizes.part
                ]
            bases[o][sizes.notes :, :] = sorted_feet[: sizes.base]
            rests[o][...] = sorted_feet[sizes.base :]


def forward_first_kernel(
    sizes, at_ref, flux_ref, got_ref, all_ref, out_ref, level_ref, feet_ref, read_ref
):
    step = pl.program_id(0)
    feet, notes, plane = first_round(sizes, got_ref, step)
    read = read_notes(sizes, notes, plane)
    feet_ref[...], read_ref[...] = feet, read
    sums = partial_sums(sizes, flux_ref, feet, read)

    @pl.when(step == 0)
    def _():
        out_ref[...] = sums
        level_ref[...] = jnp.broadcast_to(level_of(sizes, all_ref), level_ref.shape)

    @pl.when(step > 0)
    def _():
        out_ref[...] += sums


def forward_second_kernel(sizes, more, at_ref, flux_ref, before_ref, *refs):
    bases, rests, (out_ref, read_ref) = refs[: sizes.owners], refs[sizes.owners : -2], refs[-2:]
    feet, notes, plane = second_round(sizes, at_ref[2], bases, rests, not more)
    read = read_notes(sizes, notes, plane)
    read_ref[...] = read
    sums = before_ref[0] + partial_sums(sizes, flux_ref, feet, read)
    out_ref[...] = jnp.broadcast_to(sums[None], out_ref.shape)


def adjoint_kernel(sizes, at_ref, sums_ref, feet_ref, read_ref, read_second_ref, *refs):
    bases, rests = refs[: sizes.owners], refs[sizes.owners : -4]
    modeled_ref, out_ref, grad_ref, written = refs[-4:]
    sums = jnp.sum(sums_ref[...], axis=0)
    model = jnp.concatenate(thirds(sums), axis=0).astype(jnp.bfloat16)
    me = at_ref[0]
    page, within = lax.div(me, sizes.per_page), lax.rem(me, sizes.per_page)
    lane = iota((8, LANES), 1)
    own = jnp.zeros((8, LANES), jnp.float32)
    for p in range(sizes.pages):
        own = jnp.where(page == p, sums[p * 8 : (p + 1) * 8], own)
    result = jnp.zeros(modeled_ref.shape, jnp.float32)
    at_block = iota(modeled_ref.shape, 1)
    each = 8 // sizes.soundings
    for q in range(sizes.states // 8):
        picked = jnp.where(lane == q * sizes.per_page + within, own, 0.0)
        column = jnp.sum(picked, axis=1, keepdims=True)
        for n in range(each):
            values = column[n * sizes.soundings : (n + 1) * sizes.soundings]
            result = jnp.where(at_block == q * each + n, values, result)
    modeled_ref[...] = result

    pairs = [(coefficients(sizes, model, read_ref[...]), feet_ref, 0)]
    second = coefficients(sizes, model, read_second_ref[...])
    for n, ref in enumerate(bases):
        pairs.append((second[:, n * sizes.base : (n + 1) * sizes.base], ref, sizes.notes))
    if rests:
        *rests, read_more_ref = rests
        last = coefficients(sizes, model, read_more_ref[...])
        more = rests[0].shape[0]
        for n, ref in enumerate(rests):
            pairs.append((last[:, n * more : (n + 1) * more], ref, 0))
    half = sizes.part // 2 if sizes.part > LANES else sizes.part
    copies = []
    for n in range(sizes.part // half):
        lanes = slice(n * half, (n + 1) * half)
        terms = sum(
            jnp.dot(each, ref[first:, lanes], preferred_element_type=jnp.float32)
            for each, ref, first in pairs
        )
        grad_ref[:, :, lanes] = terms.reshape(sizes.hours, sizes.tiles, half)
        copies.append(
            pltpu.make_async_copy(grad_ref.at[:, :, lanes], out_ref.at[:, :, lanes], written.at[n])
        )
        copies[-1].start()
    for copy in copies:
        copy.wait()


def shards(footprint, obs_hour, tile_list, tile_row, flux, observed, obs_var):
    sizes = Sizes(
        lax.axis_size("flux"), lax.axis_size("obs"), footprint.shape, flux.shape
    )
    owners, columns, devices, part = sizes.owners, sizes.columns, sizes.devices, sizes.part
    both = ("flux", "obs")
    params = pltpu.CompilerParams(vmem_limit_bytes=VMEM_BYTES)
    me = lax.axis_index("flux") * columns + lax.axis_index("obs")
    at = jnp.stack([me, lax.axis_index("obs"), lax.axis_index("flux")])
    flux = flux.transpose(1, 0, 2)

    first_height = sizes.lane_tiles * sizes.rows + 8
    spill_height = sizes.lane_tiles * sizes.spill + 16
    all_slots = sizes.slots * sizes.per_slot
    group = columns // PACK_STEPS
    tables = (tile_list.T, tile_row, obs_hour.T, observed.T, obs_var.T)
    send, *spills = pl.pallas_call(
        functools.partial(pack_kernel, sizes),
        in_specs=[pl.BlockSpec(memory_space=pltpu.SMEM)]
        + [pl.BlockSpec(memory_space=pltpu.HBM)] * 6,
        out_specs=[pl.BlockSpec(memory_space=pltpu.HBM)] * (1 + columns),
        scratch_shapes=[
            pltpu.VMEM(
                (PACK_STEPS, all_slots // sizes.lags, sizes.lags, group * part), jnp.bfloat16
            ),
            pltpu.VMEM((PACK_STEPS, owners, group, first_height, LANES), jnp.bfloat16),
            pltpu.VMEM((PACK_STEPS, group, spill_height, LANES), jnp.bfloat16),
            pltpu.VMEM((owners, 8, LANES), jnp.float32),
            pltpu.SMEM((owners + 1,), jnp.int32),
        ]
        + [pltpu.SMEM(table.shape, table.dtype) for table in tables]
        + [pltpu.SemaphoreType.DMA((n,)) for n in (5, PACK_STEPS, PACK_STEPS, columns)],
        out_shape=[pltpu.HBM((owners, columns, first_height, LANES), jnp.bfloat16)]
        + [jax.ShapeDtypeStruct((spill_height, LANES), jnp.bfloat16)] * columns,
        compiler_params=pltpu.CompilerParams(vmem_limit_bytes=ALL_VMEM_BYTES),
        name="pack",
    )(
        at,
        *tables,
        footprint.reshape(all_slots // sizes.lags, sizes.lags, columns * part),
    )
    got = lax.all_to_all(
        send.reshape(devices, first_height, LANES), both, split_axis=0, concat_axis=0, tiled=True
    )
    mine = spills[0]
    spills = spills[:1] + [
        lax.ppermute(spills[d], "obs", [(i, i ^ d) for i in range(columns)])
        for d in range(1, columns)
    ]
    second_height = sizes.notes + sizes.second
    base_height, more_height = sizes.notes + sizes.base, sizes.second - sizes.base
    outs = [(base_height, part)] * owners + [(more_height, part)] * owners
    parts = pl.pallas_call(
        functools.partial(regroup_kernel, sizes),
        grid_spec=pltpu.PrefetchScalarGridSpec(
            num_scalar_prefetch=1,
            grid=(owners,),
            in_specs=[pl.BlockSpec((spill_height, LANES), lambda o, at: (0, 0))] * columns,
            out_specs=[pl.BlockSpec(shape, lambda o, at: (0, 0)) for shape in outs],
            scratch_shapes=[
                pltpu.VMEM((columns * sizes.spill, part), jnp.bfloat16),
                pltpu.VMEM((16, columns * sizes.spill), jnp.float32),
                pltpu.VMEM((sizes.second, columns * sizes.spill), jnp.bfloat16),
            ],
        ),
        out_shape=[jax.ShapeDtypeStruct(shape, jnp.bfloat16) for shape in outs],
        compiler_params=params,
        name="regroup",
    )(at, *spills)

    def swap(arrays):
        return arrays[:1] + [
            lax.ppermute(arrays[n], "flux", [(i, i ^ n) for i in range(owners)])
            for n in range(1, owners)
        ]

    parts = list(parts)
    bases, rests = swap(parts[:owners]), parts[owners:]

    sources = min(devices, 1024 // sizes.rows)
    chunks = devices // sources
    copies = devices if devices <= 64 else 1
    height = 8 * sizes.pages
    flux_spec = pl.BlockSpec((sizes.hours, sizes.tiles, part), lambda i, at: (0, 0, at[1]))
    base_specs = [pl.BlockSpec((base_height, part), lambda i, at: (0, 0))] * owners
    early, level, feet_first, read_first = pl.pallas_call(
        functools.partial(forward_first_kernel, sizes),
        grid_spec=pltpu.PrefetchScalarGridSpec(
            num_scalar_prefetch=1,
            grid=(chunks,),
            in_specs=[
                flux_spec,
                pl.BlockSpec((sources, first_height, LANES), lambda i, at: (i, 0, 0)),
                pl.BlockSpec((devices, 8, LANES), lambda i, at: (0, first_height // 8 - 1, 0)),
            ],
            out_specs=(
                pl.BlockSpec((height, LANES), lambda i, at: (0, 0)),
                pl.BlockSpec((8, LANES), lambda i, at: (0, 0)),
                pl.BlockSpec((sources * sizes.rows, part), lambda i, at: (i, 0)),
                pl.BlockSpec((8, sources * sizes.rows), lambda i, at: (0, i)),
            ),
        ),
        out_shape=(
            jax.ShapeDtypeStruct((height, LANES), jnp.float32),
            jax.ShapeDtypeStruct((8, LANES), jnp.int32),
            jax.ShapeDtypeStruct((devices * sizes.rows, part), jnp.bfloat16),
            jax.ShapeDtypeStruct((8, devices * sizes.rows), jnp.float32),
        ),
        compiler_params=params,
        name="forward_first",
    )(at, flux, got, got)

    smem, vmem = pl.BlockSpec(memory_space=pltpu.SMEM), pl.BlockSpec(memory_space=pltpu.VMEM)
    late_flux = lax.optimization_barrier((flux, mine))[0]
    own_flux = lax.dynamic_slice_in_dim(late_flux, lax.axis_index("obs") * part, part, axis=2)

    def forward_second(own_flux, before, bases, rests, more):
        return pl.pallas_call(
            functools.partial(forward_second_kernel, sizes, more > 0),
            in_specs=[smem] + [vmem] * (2 + len(bases) + len(rests)),
            out_specs=(vmem, vmem),
            out_shape=(
                jax.ShapeDtypeStruct((copies, height, LANES), jnp.float32),
                jax.ShapeDtypeStruct((8, owners * (more or sizes.base)), jnp.float32),
            ),
            compiler_params=params,
            name="forward_more" if more else "forward_second",
        )(at, own_flux, before, *bases, *rests)

    sums, read_second = forward_second(own_flux, early[None], bases, [], 0)
    kept = (feet_first, read_first, read_second)

    def finish(sixteenths):
        more = sizes.second * sixteenths // 16

        def run(own_flux, kept, sums, bases, rests, at):
            if more:
                rests = swap([rest[:more] for rest in rests])
                sums, read_more = forward_second(own_flux, sums, bases, rests, more)
                rests.append(read_more)
            else:
                rests = []
            if copies > 1:
                sums = lax.all_to_all(sums, both, split_axis=0, concat_axis=0, tiled=True)
            else:
                sums = lax.psum(sums, both)
            return pl.pallas_call(
                functools.partial(adjoint_kernel, sizes),
                in_specs=[smem] + [vmem] * (4 + len(bases) + len(rests)),
                out_specs=(vmem, pl.BlockSpec(memory_space=pltpu.HBM)),
                out_shape=(
                    jax.ShapeDtypeStruct((sizes.soundings, sizes.blocks), jnp.float32),
                    jax.ShapeDtypeStruct((sizes.hours, sizes.tiles, part), jnp.float32),
                ),
                scratch_shapes=[
                    pltpu.VMEM((sizes.hours, sizes.tiles, part), jnp.float32),
                    pltpu.SemaphoreType.DMA((2,)),
                ],
                compiler_params=params,
                name="adjoint",
            )(at, sums, *kept, *bases, *rests)

        return run

    modeled, gradient = lax.switch(
        level[0, 0], [finish(n) for n in REST], own_flux, kept, sums, bases, rests, at
    )
    return modeled.T, gradient.transpose(1, 0, 2)


def solution(mesh):
    placed = (
        P(("flux", "obs"), None, None, None, None),
        P(("flux", "obs"), None),
        P(("flux", "obs"), None),
        P(),
        P("flux", None, None),
        P(("flux", "obs"), None),
        P(("flux", "obs"), None),
    )
    return jax.shard_map(
        shards,
        mesh=mesh,
        in_specs=placed,
        out_specs=(P(("flux", "obs"), None), P("flux", None, "obs")),
        check_vma=False,
    )
```

time: 108 us -> 105 us (0.972)
  Pallas kernels: 24.7 us -> 21.4 us
  waiting for transfers between devices: 46 us -> 44 us
  local copies, waits for them, and re-layouts: 0.59 us -> 2.56 us
    pallas_call x2, Pallas kernels: 12 us -> 9.47 us  [the longest x1 5.24 us: run(): pl.pallas_call(functools.partial(adjoint_kernel, sizes), in_specs=[smem]...]
    all_to_all x1, waiting for transfers between devices: 5.09 us -> 3.09 us  [shards(): lax.all_to_all(send.reshape(devices, first_height, LANES), both, split_ax...]
    dynamic_slice x0 -> x1, local copies, waits for them, and re-layouts: none -> 1.99 us  [shards(): lax.dynamic_slice_in_dim(late_flux, lax.axis_index('obs') * part, part, a...]
  transfers between devices with their start and end apart: 11 -> 11, of which waited for: 6 -> 6; matrix products, arithmetic and copies ran while one was open for 0% -> 2% of each run, Pallas kernels for 9% -> 9%
where the time goes in v2:
time: 105 us
  waiting for transfers between devices  44 us (42%)
  Pallas kernels  21.4 us (20%)
  starting transfers between devices  18.9 us (18%)
  blocking collectives  16.3 us (16%)
  local copies, waits for them, and re-layouts  2.56 us (2%)
  between operations  1.41 us (1%)
    ppermute x7, waiting for transfers between devices, shards(): lax.ppermute(spills[d], 'obs', [(i, i ^ d) for i in range(columns)])  28.5 us
    all_to_all x1, blocking collectives, run(): sums = lax.all_to_all(sums, both, split_axis=0, concat_axis=0, tiled=True)  16.3 us
    ppermute x3, waiting for transfers between devices, swap(): lax.ppermute(arrays[n], 'flux', [(i, i ^ n) for i in range(owners)])  12.4 us
    all_to_all x1, starting transfers between devices, shards(): lax.all_to_all(send.reshape(devices, first_height, LANES), both, split_ax...  7.3 us
    ppermute x7, starting transfers between devices, shards(): lax.ppermute(spills[d], 'obs', [(i, i ^ d) for i in range(columns)])  6.71 us
    pallas_call x1, Pallas kernels, shards(): pl.pallas_call(functools.partial(regroup_kernel, sizes), grid_spec=pltpu....  5.85 us
    pallas_call x1, Pallas kernels, run(): pl.pallas_call(functools.partial(adjoint_kernel, sizes), in_specs=[smem]...  5.24 us
    ppermute x3, starting transfers between devices, swap(): lax.ppermute(arrays[n], 'flux', [(i, i ^ n) for i in range(owners)])  4.87 us
  transfers between devices with their start and end apart: 11, of which 6 were waited for; matrix products, arithmetic and copies ran while one was open for 2% of the time, Pallas kernels for 9%

profile of v2, /device:TPU:0, one launch (start us, length us, event | category | flops | bytes accessed | tf_op | source)
XLA Modules:
  0.0 104.6 jit_solution(2746655644384530832)
XLA Ops:
  0.6 0.1 pad_add_fusion.at_ref
  0.7 4.2 %pack.1 = (bf16[4,8,264,128]{3,2,1,0:T(8,128)(2,1)}, bf16[528,128]{1,0:T(8,128)(2,1)}, bf16[528,128]{1,0:T(8,128)(2,1)}, bf16[528,128]{1,0:T(8,128)(2,1)}, bf16[...) custom-call(s32[3]{0:T(128)S(1)} %pad_add_fusion.at_ref, ...), custom_call_target="tpu_custom_call" | custom-call | tf_op jit(solution)/shard_map/pack/pallas_call | solution.py:439
  5.0 0.0 copy-start.13
  5.0 0.0 copy-start.12
  5.0 0.0 copy-start.11
  5.0 0.0 copy-start.10
  5.0 0.0 copy-start.9
  5.0 0.0 copy-start.8
  5.0 0.0 copy-start.7
  5.0 0.0 copy-start
  5.0 7.3 %all-to-all-start.3 = ((bf16[32,264,128]{2,1,0:T(8,128)(2,1)}), bf16[32,264,128]{2,1,0:T(8,128)(2,1)S(1)}, u32[]{:S(2)}, u32[]{:S(2)}) async-start(bf16[32,264,128]{2,1,0:T(8,128)(2,1)} %bitcast.17), calls=%async_computation.3 | async-start | bytes 4325376 | tf_op jit(solution)/shard_map/all_to_all | solution.py:464
  12.3 0.0 copy-done.13
  12.4 0.3 collective-permute-start.6
  12.7 0.0 copy-done.12
  12.7 1.7 %collective-permute-start.7 = (bf16[528,128]{1,0:T(8,128)(2,1)S(1)}, bf16[528,128]{1,0:T(8,128)(2,1)S(1)}, u32[]{:S(2)}, u32[]{:S(2)}) collective-permute-start(bf16[528,128]{1,0:T(8,128)(2,1)S(1)} %copy-done.12), channel_id=1, source_target_pairs={{0,2},{1,3},{2,0},{3,1},{4,6},{5,7},{6,4},{7,5},{8,10},{9,11},{10,... | collective-permute-start | bytes 405512 | tf_op jit(solution)/shard_map/ppermute | solution.py:469
  14.4 0.0 copy-done.11
  14.4 0.0 collective-permute-start.8
  14.4 0.0 copy-done.10
  14.4 1.7 %collective-permute-start.9 = (bf16[528,128]{1,0:T(8,128)(2,1)S(1)}, bf16[528,128]{1,0:T(8,128)(2,1)S(1)}, u32[]{:S(2)}, u32[]{:S(2)}) collective-permute-start(bf16[528,128]{1,0:T(8,128)(2,1)S(1)} %copy-done.10), channel_id=1, source_target_pairs={{0,4},{1,5},{2,6},{3,7},{4,0},{5,1},{6,2},{7,3},{8,12},{9,13},{10,... | collective-permute-start | bytes 405512 | tf_op jit(solution)/shard_map/ppermute | solution.py:469
  16.1 0.0 copy-done.9
  16.1 0.1 collective-permute-start.10
  16.2 0.0 collective-permute-done.6.refs_1_
  16.2 0.0 copy-done.8
  16.2 2.6 %collective-permute-start.11 = (bf16[528,128]{1,0:T(8,128)(2,1)S(1)}, bf16[528,128]{1,0:T(8,128)(2,1)S(1)}, u32[]{:S(2)}, u32[]{:S(2)}) collective-permute-start(bf16[528,128]{1,0:T(8,128)(2,1)S(1)} %copy-done.8), channel_id=1, source_target_pairs={{0,6},{1,7},{2,4},{3,5},{4,2},{5,3},{6,0},{7,1},{8,14},{9,15},{10,... | collective-permute-start | bytes 405512 | tf_op jit(solution)/shard_map/ppermute | solution.py:469
  18.8 13.5 %collective-permute-done.7.refs_2_ = bf16[528,128]{1,0:T(8,128)(2,1)S(1)} collective-permute-done((bf16[528,128]{1,0:T(8,128)(2,1)S(1)}, bf16[528,128]{1,0:T(8,128)(2,1)S(1)}, u32[]{:S(2)}, u32[]{:S(2)}) %collective-permute-start.7) | collective-permute-done | bytes 135200 | tf_op jit(solution)/shard_map/ppermute | solution.py:469
  32.2 0.0 copy-done.7
  32.2 0.3 collective-permute-start.12
  32.6 4.5 %collective-permute-done.8.refs_3_ = bf16[528,128]{1,0:T(8,128)(2,1)S(1)} collective-permute-done((bf16[528,128]{1,0:T(8,128)(2,1)S(1)}, bf16[528,128]{1,0:T(8,128)(2,1)S(1)}, u32[]{:S(2)}, u32[]{:S(2)}) %collective-permute-start.8) | collective-permute-done | bytes 135200 | tf_op jit(solution)/shard_map/ppermute | solution.py:469
  37.1 0.0 collective-permute-done.9.refs_4_
  37.1 0.0 collective-permute-done.10.refs_5_
  37.1 8.3 %collective-permute-done.11.refs_6_ = bf16[528,128]{1,0:T(8,128)(2,1)S(1)} collective-permute-done((bf16[528,128]{1,0:T(8,128)(2,1)S(1)}, bf16[528,128]{1,0:T(8,128)(2,1)S(1)}, u32[]{:S(2)}, u32[]{:S(2)}) %collective-permute-start.11) | collective-permute-done | bytes 135200 | tf_op jit(solution)/shard_map/ppermute | solution.py:469
  45.4 2.2 %collective-permute-done.12.refs_7_ = bf16[528,128]{1,0:T(8,128)(2,1)S(1)} collective-permute-done((bf16[528,128]{1,0:T(8,128)(2,1)S(1)}, bf16[528,128]{1,0:T(8,128)(2,1)S(1)}, u32[]{:S(2)}, u32[]{:S(2)}) %collective-permute-start.12) | collective-permute-done | bytes 135200 | tf_op jit(solution)/shard_map/ppermute | solution.py:469
  47.6 0.0 copy-done
  47.6 5.8 %regroup.1 = (bf16[264,512]{1,0:T(8,128)(2,1)S(1)}, bf16[264,512]{1,0:T(8,128)(2,1)S(1)}, bf16[264,512]{1,0:T(8,128)(2,1)S(1)}, bf16[264,512]{1,0:T(8,128)(2,1)S...) custom-call(s32[3]{0:T(128)S(1)} %pad_add_fusion.at_ref, ...), custom_call_target="tpu_custom_call" | custom-call | tf_op jit(solution)/shard_map/regroup/pallas_call | solution.py:475
  53.5 0.6 collective-permute-start.13
  54.1 4.2 %collective-permute-start.14 = (bf16[264,512]{1,0:T(8,128)(2,1)S(1)}, bf16[264,512]{1,0:T(8,128)(2,1)}, u32[]{:S(2)}, u32[]{:S(2)}) collective-permute-start(bf16[264,512]{1,0:T(8,128)(2,1)S(1)} %get-tuple-element.157), channel_id=1, source_target_pairs={{0,16},{8,24},{16,0},{24,8},{1,17},{9,25},{17,1},{25,9},{2,18},{10... | collective-permute-start | bytes 811016 | tf_op jit(solution)/shard_map/ppermute | solution.py:495
  58.3 0.0 collective-permute-start.15
  58.3 2.0 %constant_dynamic-slice_fusion.flux_ref = bf16[5,128,512]{2,1,0:T(8,128)(2,1)} fusion(bf16[5,128,4096]{2,1,0:T(8,128)(2,1)} %bitcast.15, s32[]{:T(128)S(6)} %select_n.3), kind=kLoop, calls=%fused_computation.1 | loop fusion | bytes 1310724 | tf_op jit(solution)/shard_map/dynamic_slice | solution.py:537
  60.3 3.1 %all-to-all-done.3.got_ref.all_ref = bf16[32,264,128]{2,1,0:T(8,128)(2,1)S(1)} async-done(((bf16[32,264,128]{2,1,0:T(8,128)(2,1)}), bf16[32,264,128]{2,1,0:T(8,128)(2,1)S(1)}, u32[]{:S(2)}, u32[]{:S(2)}) %all-to-all-start.3) | async-done | bytes 2162720 | tf_op jit(solution)/shard_map/all_to_all | solution.py:464
  63.4 0.0 copy-start.5
  63.4 3.9 %forward_first.1 = (f32[8,128]{1,0:T(8,128)S(1)}, s32[8,128]{1,0:T(8,128)S(1)}, bf16[2048,512]{1,0:T(8,128)(2,1)S(1)}, f32[8,2048]{1,0:T(8,128)S(1)}) custom-call(s32[3]{0:T(128)S(1)} %pad_add_fusion.at_ref, bf16[5,128,4096]{2,1,0:T(8,128)(2,1)} %bitcast.16, bf16[32,264,128]{2,1,0:T(8,128)(2,1)S(1)} %all-to-all-done.3.got_ref.all_ref, ...), custom_call_target="tpu_custom_call" | custom-call | tf_op jit(solution)/shard_map/forward_first/pallas_call | solution.py:508
  67.3 0.5 slice.15
  68.5 0.0 collective-permute-done.13.refs_1_
  68.5 12.4 %collective-permute-done.14.refs_2_ = bf16[264,512]{1,0:T(8,128)(2,1)} collective-permute-done((bf16[264,512]{1,0:T(8,128)(2,1)S(1)}, bf16[264,512]{1,0:T(8,128)(2,1)}, u32[]{:S(2)}, u32[]{:S(2)}) %collective-permute-start.14) | collective-permute-done | bytes 270368 | tf_op jit(solution)/shard_map/ppermute | solution.py:495
  80.8 0.0 collective-permute-done.15.refs_3_
  80.8 0.0 copy-done.5
  80.8 2.2 %forward_second.1 = (f32[32,8,128]{2,1,0:T(8,128)S(1)}, f32[8,1024]{1,0:T(8,128)S(1)}) custom-call(s32[3]{0:T(128)S(1)} %pad_add_fusion.at_ref, bf16[5,128,512]{2,1,0:T(8,128)(2,1)S(1)} %copy-done.5, f32[1,8,128]{2,1,0:T(8,128)S(1)} %bitcast.14, bf16[264,512]{1,0:T(8,128)(2,1)S(1)} %get-tuple-element.155.refs_0_, ...), custom_call_target="tpu_custom_call" | custom-call | tf_op jit(solution)/shard_map/forward_second/pallas_call | solution.py:540
  83.1 21.5 %conditional.1 = ((f32[4,8]{1,0:T(4,128)}, f32[5,128,512]{2,1,0:T(8,128)})) conditional(s32[]{:T(128)} %bitcast.10, (f32[32,8,128]{2,1,0:T(8,128)S(1)}, s32[3]{0:T(128)S(1)}, bf16[2048,512]{1,0:T(8,128)(2,1)S(1)}, f32[8,2048]{1,0:T(8,128)S(1)}, f32[8,1024]{1,0:T(8,128)S(1)}, /*index=5*/bf16[264,512]{1,0:T(8,128)(2,1)S(1)}, ...), branch_computations={%region_0.0_spmd, %region_1.0_spmd, %region_2.0_spmd} | conditional | bytes 21233876 | solution.py:587
  83.1 16.3 %all_to_all.17.sums_ref = f32[32,8,128]{2,1,0:T(8,128)S(1)} all-to-all(f32[32,8,128]{2,1,0:T(8,128)S(1)} %get-tuple-element.75), channel_id=1, replica_groups=mesh['flux'=4,'obs'=8] {'flux','obs'}, dimensions={0} | all-to-all | bytes 262144 | tf_op jit(solution)/shard_map/cond/branch_0_fun/all_to_all | solution.py:566
  99.4 5.2 %adjoint.3 = (f32[4,8]{1,0:T(4,128)}, f32[5,128,512]{2,1,0:T(8,128)}) custom-call(s32[3]{0:T(128)S(1)} %get-tuple-element.74.at_ref, f32[32,8,128]{2,1,0:T(8,128)S(1)} %all_to_all.17.sums_ref, bf16[2048,512]{1,0:T(8,128)(2,1)S(1)} %get-tuple-element.76.feet_ref, f32[8,2048]{1,0:T(8,128)S(1)} %get-tuple-element.77.read_ref, ...), custom_call_target="tpu_custom_call" | custom-call | tf_op jit(solution)/shard_map/cond/branch_0_fun/adjoint/pallas_call | solution.py:569
Async XLA Ops:
  5.0 7.4 %copy-start.13 = (bf16[528,128]{1,0:T(8,128)(2,1)S(1)}, bf16[528,128]{1,0:T(8,128)(2,1)}, u32[]{:S(2)}) copy-start(bf16[528,128]{1,0:T(8,128)(2,1)} %get-tuple-element.148) | copy-start | bytes 405508
  5.0 7.7 %copy-start.12 = (bf16[528,128]{1,0:T(8,128)(2,1)S(1)}, bf16[528,128]{1,0:T(8,128)(2,1)}, u32[]{:S(2)}) copy-start(bf16[528,128]{1,0:T(8,128)(2,1)} %get-tuple-element.149) | copy-start | bytes 405508
  5.0 9.4 %copy-start.11 = (bf16[528,128]{1,0:T(8,128)(2,1)S(1)}, bf16[528,128]{1,0:T(8,128)(2,1)}, u32[]{:S(2)}) copy-start(bf16[528,128]{1,0:T(8,128)(2,1)} %get-tuple-element.150) | copy-start | bytes 405508
  5.0 9.4 %copy-start.10 = (bf16[528,128]{1,0:T(8,128)(2,1)S(1)}, bf16[528,128]{1,0:T(8,128)(2,1)}, u32[]{:S(2)}) copy-start(bf16[528,128]{1,0:T(8,128)(2,1)} %get-tuple-element.151) | copy-start | bytes 405508
  5.0 11.1 %copy-start.9 = (bf16[528,128]{1,0:T(8,128)(2,1)S(1)}, bf16[528,128]{1,0:T(8,128)(2,1)}, u32[]{:S(2)}) copy-start(bf16[528,128]{1,0:T(8,128)(2,1)} %get-tuple-element.152) | copy-start | bytes 405508
  5.0 11.2 %copy-start.8 = (bf16[528,128]{1,0:T(8,128)(2,1)S(1)}, bf16[528,128]{1,0:T(8,128)(2,1)}, u32[]{:S(2)}) copy-start(bf16[528,128]{1,0:T(8,128)(2,1)} %get-tuple-element.153) | copy-start | bytes 405508
  5.0 27.2 %copy-start.7 = (bf16[528,128]{1,0:T(8,128)(2,1)S(1)}, bf16[528,128]{1,0:T(8,128)(2,1)}, u32[]{:S(2)}) copy-start(bf16[528,128]{1,0:T(8,128)(2,1)} %get-tuple-element.154) | copy-start | bytes 405508
  5.0 42.6 %copy-start = (bf16[528,128]{1,0:T(8,128)(2,1)S(1)}, bf16[528,128]{1,0:T(8,128)(2,1)}, u32[]{:S(2)}) copy-start(bf16[528,128]{1,0:T(8,128)(2,1)} %get-tuple-element.145.refs_0_) | copy-start | bytes 405508
  5.0 58.4 %all-to-all-start.3 = ((bf16[32,264,128]{2,1,0:T(8,128)(2,1)}), bf16[32,264,128]{2,1,0:T(8,128)(2,1)S(1)}, u32[]{:S(2)}, u32[]{:S(2)}) async-start(bf16[32,264,128]{2,1,0:T(8,128)(2,1)} %bitcast.17), calls=%async_computation.3 | async-start | bytes 4325376 | tf_op jit(solution)/shard_map/all_to_all | solution.py:464
  12.4 3.8 %collective-permute-start.6 = (bf16[528,128]{1,0:T(8,128)(2,1)S(1)}, bf16[528,128]{1,0:T(8,128)(2,1)S(1)}, u32[]{:S(2)}, u32[]{:S(2)}) collective-permute-start(bf16[528,128]{1,0:T(8,128)(2,1)S(1)} %copy-done.13), channel_id=1, source_target_pairs={{0,1},{1,0},{2,3},{3,2},{4,5},{5,4},{6,7},{7,6},{8,9},{9,8},{10,11... | collective-permute-start | bytes 405512 | tf_op jit(solution)/shard_map/ppermute | solution.py:469
  12.7 19.6 %collective-permute-start.7 = (bf16[528,128]{1,0:T(8,128)(2,1)S(1)}, bf16[528,128]{1,0:T(8,128)(2,1)S(1)}, u32[]{:S(2)}, u32[]{:S(2)}) collective-permute-start(bf16[528,128]{1,0:T(8,128)(2,1)S(1)} %copy-done.12), channel_id=1, source_target_pairs={{0,2},{1,3},{2,0},{3,1},{4,6},{5,7},{6,4},{7,5},{8,10},{9,11},{10,... | collective-permute-start | bytes 405512 | tf_op jit(solution)/shard_map/ppermute | solution.py:469
  14.4 22.7 %collective-permute-start.8 = (bf16[528,128]{1,0:T(8,128)(2,1)S(1)}, bf16[528,128]{1,0:T(8,128)(2,1)S(1)}, u32[]{:S(2)}, u32[]{:S(2)}) collective-permute-start(bf16[528,128]{1,0:T(8,128)(2,1)S(1)} %copy-done.11), channel_id=1, source_target_pairs={{0,3},{1,2},{2,1},{3,0},{4,7},{5,6},{6,5},{7,4},{8,11},{9,10},{10,... | collective-permute-start | bytes 405512 | tf_op jit(solution)/shard_map/ppermute | solution.py:469
  14.4 22.7 %collective-permute-start.9 = (bf16[528,128]{1,0:T(8,128)(2,1)S(1)}, bf16[528,128]{1,0:T(8,128)(2,1)S(1)}, u32[]{:S(2)}, u32[]{:S(2)}) collective-permute-start(bf16[528,128]{1,0:T(8,128)(2,1)S(1)} %copy-done.10), channel_id=1, source_target_pairs={{0,4},{1,5},{2,6},{3,7},{4,0},{5,1},{6,2},{7,3},{8,12},{9,13},{10,... | collective-permute-start | bytes 405512 | tf_op jit(solution)/shard_map/ppermute | solution.py:469
  16.1 21.0 %collective-permute-start.10 = (bf16[528,128]{1,0:T(8,128)(2,1)S(1)}, bf16[528,128]{1,0:T(8,128)(2,1)S(1)}, u32[]{:S(2)}, u32[]{:S(2)}) collective-permute-start(bf16[528,128]{1,0:T(8,128)(2,1)S(1)} %copy-done.9), channel_id=1, source_target_pairs={{0,5},{1,4},{2,7},{3,6},{4,1},{5,0},{6,3},{7,2},{8,13},{9,12},{10,... | collective-permute-start | bytes 405512 | tf_op jit(solution)/shard_map/ppermute | solution.py:469
  16.2 29.2 %collective-permute-start.11 = (bf16[528,128]{1,0:T(8,128)(2,1)S(1)}, bf16[528,128]{1,0:T(8,128)(2,1)S(1)}, u32[]{:S(2)}, u32[]{:S(2)}) collective-permute-start(bf16[528,128]{1,0:T(8,128)(2,1)S(1)} %copy-done.8), channel_id=1, source_target_pairs={{0,6},{1,7},{2,4},{3,5},{4,2},{5,3},{6,0},{7,1},{8,14},{9,15},{10,... | collective-permute-start | bytes 405512 | tf_op jit(solution)/shard_map/ppermute | solution.py:469
  32.2 15.3 %collective-permute-start.12 = (bf16[528,128]{1,0:T(8,128)(2,1)S(1)}, bf16[528,128]{1,0:T(8,128)(2,1)S(1)}, u32[]{:S(2)}, u32[]{:S(2)}) collective-permute-start(bf16[528,128]{1,0:T(8,128)(2,1)S(1)} %copy-done.7), channel_id=1, source_target_pairs={{0,7},{1,6},{2,5},{3,4},{4,3},{5,2},{6,1},{7,0},{8,15},{9,14},{10,... | collective-permute-start | bytes 405512 | tf_op jit(solution)/shard_map/ppermute | solution.py:469
  53.5 15.0 %collective-permute-start.13 = (bf16[264,512]{1,0:T(8,128)(2,1)S(1)}, bf16[264,512]{1,0:T(8,128)(2,1)}, u32[]{:S(2)}, u32[]{:S(2)}) collective-permute-start(bf16[264,512]{1,0:T(8,128)(2,1)S(1)} %get-tuple-element.156), channel_id=1, source_target_pairs={{0,8},{8,0},{16,24},{24,16},{1,9},{9,1},{17,25},{25,17},{2,10},{10... | collective-permute-start | bytes 811016 | tf_op jit(solution)/shard_map/ppermute | solution.py:495
  54.1 26.7 %collective-permute-start.14 = (bf16[264,512]{1,0:T(8,128)(2,1)S(1)}, bf16[264,512]{1,0:T(8,128)(2,1)}, u32[]{:S(2)}, u32[]{:S(2)}) collective-permute-start(bf16[264,512]{1,0:T(8,128)(2,1)S(1)} %get-tuple-element.157), channel_id=1, source_target_pairs={{0,16},{8,24},{16,0},{24,8},{1,17},{9,25},{17,1},{25,9},{2,18},{10... | collective-permute-start | bytes 811016 | tf_op jit(solution)/shard_map/ppermute | solution.py:495
  58.3 22.5 %collective-permute-start.15 = (bf16[264,512]{1,0:T(8,128)(2,1)S(1)}, bf16[264,512]{1,0:T(8,128)(2,1)}, u32[]{:S(2)}, u32[]{:S(2)}) collective-permute-start(bf16[264,512]{1,0:T(8,128)(2,1)S(1)} %get-tuple-element.158), channel_id=1, source_target_pairs={{0,24},{8,16},{16,8},{24,0},{1,25},{9,17},{17,9},{25,1},{2,26},{10... | collective-permute-start | bytes 811016 | tf_op jit(solution)/shard_map/ppermute | solution.py:495
  63.4 17.4 %copy-start.5 = (bf16[5,128,512]{2,1,0:T(8,128)(2,1)S(1)}, bf16[5,128,512]{2,1,0:T(8,128)(2,1)}, u32[]{:S(2)}) copy-start(bf16[5,128,512]{2,1,0:T(8,128)(2,1)} %constant_dynamic-slice_fusion.flux_ref) | copy-start | bytes 1966084

commit v3 on v2

--- a/solution.py
+++ b/solution.py
@@ -10,8 +10,8 @@
 LANES = 128
 VMEM_BYTES = 48 * 1024 * 1024
 ALL_VMEM_BYTES = 60 * 1024 * 1024
-BASE = 8
-REST = (0, 2, 8)
+BASE = 256
+REST = (0, 64, 128)
 PACK_STEPS = 2
 
 
@@ -38,12 +38,17 @@
         self.per_slot = self.soundings * self.lags
         self.part = cells // columns
         self.lane_tiles = self.part // LANES
-        self.first = self.slots // owners
+        capacity = 2 * self.slots // owners
+        self.first = capacity // 2 - capacity // 16
         self.rows = self.first * self.per_slot
-        self.spill = self.slots // 2 * self.per_slot
-        self.second = columns * self.first * self.per_slot
-        self.base = self.second * BASE // 16
-        self.notes = 8 * (self.second // self.part)
+        self.spill = (self.slots - owners // 2 * self.first) * self.per_slot
+        self.spill_notes = -(-self.spill // LANES)
+        self.second = columns * (capacity - self.first) * self.per_slot
+        self.base = min(BASE, self.second)
+        self.rest = self.second - self.base
+        self.base_notes = 8 * -(-self.base // self.part)
+        self.rest_notes = 8 * -(-self.rest // self.part)
+        self.levels = tuple(n for n in REST if n < self.rest) + (self.rest,)
         self.states = self.blocks * self.soundings
         self.per_page = 8 * LANES // self.states
         self.pages = self.devices // self.per_page
@@ -85,26 +90,17 @@
     return feet, notes, plane
 
 
-def second_round(sizes, flux_index, bases, rests, with_bases=True):
+def second_round(sizes, flux_index, refs, heights):
+    count = refs[0].shape[0] - heights
     notes = [
         jnp.concatenate(
-            [ref[n * 8 : (n + 1) * 8, :].astype(jnp.float32) for n in range(sizes.notes // 8)],
-            axis=1,
-        )
-        for ref in bases
+            [ref[n * 8 : (n + 1) * 8, :].astype(jnp.float32) for n in range(heights // 8)], axis=1
+        )[:, :count]
+        for ref in refs
     ]
-    feet, kept, planes = [], [], []
-    if with_bases:
-        feet += [ref[sizes.notes :, :] for ref in bases]
-        kept += [each[:, : sizes.base] for each in notes]
-        planes.append(lax.div(iota((1, len(bases) * sizes.base), 1), jnp.int32(sizes.base)))
-    if rests:
-        more = rests[0].shape[0]
-        feet += [ref[...] for ref in rests]
-        kept += [each[:, sizes.base : sizes.base + more] for each in notes]
-        planes.append(lax.div(iota((1, len(rests) * more), 1), jnp.int32(more)))
-    plane = lax.bitwise_xor(jnp.concatenate(planes, axis=1), flux_index)
-    return jnp.concatenate(feet, axis=0), jnp.concatenate(kept, axis=1), plane
+    plane = lax.div(iota((1, len(refs) * count), 1), jnp.int32(count))
+    feet = jnp.concatenate([ref[heights:, :] for ref in refs], axis=0)
+    return feet, jnp.concatenate(notes, axis=1), lax.bitwise_xor(plane, flux_index)
 
 
 def partial_sums(sizes, flux_ref, feet, read):
@@ -182,7 +178,7 @@
         count[o] = 0
         first_notes[o] = empty[:8]
     count[owners] = 0
-    left = empty
+    lefts = [empty] * sizes.spill_notes
     for b in range(sizes.blocks):
         base = jnp.zeros(field.shape, jnp.float32)
         seen = jnp.zeros(field.shape, jnp.float32)
@@ -217,7 +213,12 @@
             first_notes[owner] = jnp.where(
                 slot_at[:8] == jnp.where(keep, position, -1), value[:8], first_notes[owner]
             )
-            left = jnp.where(slot_at == jnp.where(keep, -1, over), value, left)
+            lefts = [
+                jnp.where(
+                    slot_at + n * (LANES // per_slot) == jnp.where(keep, -1, over), value, left
+                )
+                for n, left in enumerate(lefts)
+            ]
             key = jnp.where(
                 key_at // per_slot == b * sizes.width + k,
                 goes * per_slot + key_at % per_slot,
@@ -241,19 +242,23 @@
             place,
             feet[i].reshape(key.shape[1], group * sizes.part),
             preferred_element_type=jnp.float32,
-        ).astype(jnp.bfloat16)
+        )
         for c in range(group):
             for o in range(owners):
                 for n in range(tiles):
                     lanes = slice((c * tiles + n) * LANES, (c * tiles + n + 1) * LANES)
                     sent[i, o, c, n * rows : (n + 1) * rows, :] = packed[
                         o * rows : (o + 1) * rows, lanes
-                    ]
+                    ].astype(jnp.bfloat16)
                 sent[i, o, c, end : end + 8, :] = first_notes[o].astype(jnp.bfloat16)
             for n in range(tiles):
                 lanes = slice((c * tiles + n) * LANES, (c * tiles + n + 1) * LANES)
-                spilled[i, c, n * spill : (n + 1) * spill, :] = packed[owners * rows :, lanes]
-            spilled[i, c, tiles * spill :, :] = left.astype(jnp.bfloat16)
+                spilled[i, c, n * spill : (n + 1) * spill, :] = packed[
+                    owners * rows :, lanes
+                ].astype(jnp.bfloat16)
+            for n, left in enumerate(lefts):
+                first_note = tiles * spill + n * 16
+                spilled[i, c, first_note : first_note + 16, :] = left.astype(jnp.bfloat16)
         stores.append(
             pltpu.make_async_copy(
                 sent.at[i], send_ref.at[:, pl.ds(first, group)], sent_done.at[i]
@@ -281,66 +286,52 @@
     counts = jnp.where((lane >= sizes.rows) & (lane < sizes.rows + sizes.owners), counts, 0.0)
     most = jnp.max(counts, axis=1, keepdims=True) * sizes.per_slot
     level = jnp.zeros((1, 1), jnp.int32)
-    for n in REST[:-1]:
-        level = level + jnp.where(most > sizes.base + sizes.second * n // 16, 1, 0)
+    for n in sizes.levels[:-1]:
+        level = level + jnp.where(most > sizes.base + n, 1, 0)
     return level
 
 
-def regroup_kernel(sizes, at_ref, *refs):
+def regroup_kernel(sizes, start, count, heights, at_ref, *refs):
     columns, owners, spill = sizes.columns, sizes.owners, sizes.spill
-    spills, bases = refs[:columns], refs[columns : columns + owners]
-    rests = refs[columns + owners : columns + 2 * owners]
-    feet, notes, place = refs[columns + 2 * owners :]
-    step = pl.program_id(0)
-    owner = at_ref[2] ^ step
+    spills, outs, (feet,) = refs[:columns], refs[columns : columns + owners], refs[-1:]
     end = sizes.lane_tiles * spill
-
-    @pl.when(step == 0)
-    def _():
-        for d, ref in enumerate(spills):
-            for n in range(sizes.lane_tiles):
-                feet[d * spill : (d + 1) * spill, n * LANES : (n + 1) * LANES] = ref[
-                    n * spill : (n + 1) * spill, :
-                ]
-            notes[:, d * spill : (d + 1) * spill] = ref[end : end + 16, :].astype(jnp.float32)
-
-    mine = notes[8:9, :] == owner.astype(jnp.float32)
-    total = jnp.zeros((1, 1), jnp.float32)
-    keys = []
-    for d in range(columns):
-        here = mine[:, d * spill : (d + 1) * spill]
-        position = total + notes[9:10, d * spill : (d + 1) * spill]
-        inner = lax.rem(iota((1, spill), 1), jnp.int32(sizes.per_slot))
-        keys.append(
-            jnp.where(here, position.astype(jnp.int32) * sizes.per_slot + inner, -1)
-        )
-        total = total + jnp.sum(
-            jnp.where(here, 1.0 / sizes.per_slot, 0.0), axis=1, keepdims=True
-        )
-    key = jnp.concatenate(keys, axis=1)
-    place[...] = (iota(place.shape, 0) == key).astype(jnp.bfloat16)
-    sorted_feet = jnp.dot(place[...], feet[...], preferred_element_type=jnp.float32)
-    sorted_feet = sorted_feet.astype(jnp.bfloat16)
-    moved = lax.dot_general(
-        notes[0:8, :].astype(jnp.bfloat16),
-        place[...],
-        (((1,), (1,)), ((), ())),
-        preferred_element_type=jnp.float32,
-    )
-    field, lane = iota(moved.shape, 0), iota(moved.shape, 1)
-    empty = jnp.where(field == 0, jnp.float32(sizes.half), jnp.where(field == 5, 1.0, 0.0))
-    moved = jnp.where(lane.astype(jnp.float32) < total * sizes.per_slot, moved, empty)
-    moved = moved.astype(jnp.bfloat16)
-    for o in range(owners):
-
-        @pl.when(step == o)
-        def _():
-            for n in range(sizes.notes // 8):
-                bases[o][n * 8 : (n + 1) * 8, :] = moved[
-                    :, n * sizes.part : (n + 1) * sizes.part
-                ]
-            bases[o][sizes.notes :, :] = sorted_feet[: sizes.base]
-            rests[o][...] = sorted_feet[sizes.base :]
+    notes = []
+    for d, ref in enumerate(spills):
+        for n in range(sizes.lane_tiles):
+            feet[d * spill : (d + 1) * spill, n * LANES : (n + 1) * LANES] = ref[
+                n * spill : (n + 1) * spill, :
+            ]
+        blocks = [
+            ref[end + n * 16 : end + (n + 1) * 16, :].astype(jnp.float32)
+            for n in range(sizes.spill_notes)
+        ]
+        notes.append(jnp.concatenate(blocks, axis=1)[:, :spill])
+    owner_at = jnp.concatenate([each[8:9] for each in notes], axis=0)
+    position = jnp.concatenate([each[9:10] for each in notes], axis=0).astype(jnp.int32)
+    inner = lax.rem(iota(position.shape, 1), jnp.int32(sizes.per_slot))
+    fields = jnp.concatenate([each[0:8] for each in notes], axis=1).astype(jnp.bfloat16)
+    for n in range(owners):
+        mine = owner_at == (at_ref[2] ^ n).astype(jnp.float32)
+        counts = jnp.sum(jnp.where(mine, 1.0, 0.0), axis=1, keepdims=True).astype(jnp.int32)
+        keys, total = [], jnp.zeros((1, 1), jnp.int32)
+        for d in range(columns):
+            row = total + position[d : d + 1] * sizes.per_slot + inner[d : d + 1] - start
+            keys.append(jnp.where(mine[d : d + 1], row, -1))
+            total = total + counts[d : d + 1]
+        key = jnp.concatenate(keys, axis=1)
+        place = (iota((count, columns * spill), 0) == key).astype(jnp.bfloat16)
+        outs[n][heights:, :] = jnp.dot(
+            place, feet[...], preferred_element_type=jnp.float32
+        ).astype(jnp.bfloat16)
+        moved = lax.dot_general(
+            fields, place, (((1,), (1,)), ((), ())), preferred_element_type=jnp.float32
+        )
+        field, lane = iota(moved.shape, 0), iota(moved.shape, 1)
+        empty = jnp.where(field == 0, jnp.float32(sizes.half), jnp.where(field == 5, 1.0, 0.0))
+        moved = jnp.where(lane + start < total, moved, empty)
+        for m in range(heights // 8):
+            lanes = moved[:, m * sizes.part : (m + 1) * sizes.part].astype(jnp.bfloat16)
+            outs[n][m * 8 : (m + 1) * 8, : lanes.shape[1]] = lanes
 
 
 def forward_first_kernel(
@@ -362,9 +353,9 @@
         out_ref[...] += sums
 
 
-def forward_second_kernel(sizes, more, at_ref, flux_ref, before_ref, *refs):
-    bases, rests, (out_ref, read_ref) = refs[: sizes.owners], refs[sizes.owners : -2], refs[-2:]
-    feet, notes, plane = second_round(sizes, at_ref[2], bases, rests, not more)
+def forward_second_kernel(sizes, heights, at_ref, flux_ref, before_ref, *refs):
+    *parts, out_ref, read_ref = refs
+    feet, notes, plane = second_round(sizes, at_ref[2], parts, heights)
     read = read_notes(sizes, notes, plane)
     read_ref[...] = read
     sums = before_ref[0] + partial_sums(sizes, flux_ref, feet, read)
@@ -396,13 +387,13 @@
     pairs = [(coefficients(sizes, model, read_ref[...]), feet_ref, 0)]
     second = coefficients(sizes, model, read_second_ref[...])
     for n, ref in enumerate(bases):
-        pairs.append((second[:, n * sizes.base : (n + 1) * sizes.base], ref, sizes.notes))
+        pairs.append((second[:, n * sizes.base : (n + 1) * sizes.base], ref, sizes.base_notes))
     if rests:
         *rests, read_more_ref = rests
         last = coefficients(sizes, model, read_more_ref[...])
-        more = rests[0].shape[0]
+        more = rests[0].shape[0] - sizes.rest_notes
         for n, ref in enumerate(rests):
-            pairs.append((last[:, n * more : (n + 1) * more], ref, 0))
+            pairs.append((last[:, n * more : (n + 1) * more], ref, sizes.rest_notes))
     half = sizes.part // 2 if sizes.part > LANES else sizes.part
     copies = []
     for n in range(sizes.part // half):
@@ -432,7 +423,7 @@
     flux = flux.transpose(1, 0, 2)
 
     first_height = sizes.lane_tiles * sizes.rows + 8
-    spill_height = sizes.lane_tiles * sizes.spill + 16
+    spill_height = sizes.lane_tiles * sizes.spill + sizes.spill_notes * 16
     all_slots = sizes.slots * sizes.per_slot
     group = columns // PACK_STEPS
     tables = (tile_list.T, tile_row, obs_hour.T, observed.T, obs_var.T)
@@ -469,26 +460,19 @@
         lax.ppermute(spills[d], "obs", [(i, i ^ d) for i in range(columns)])
         for d in range(1, columns)
     ]
-    second_height = sizes.notes + sizes.second
-    base_height, more_height = sizes.notes + sizes.base, sizes.second - sizes.base
-    outs = [(base_height, part)] * owners + [(more_height, part)] * owners
-    parts = pl.pallas_call(
-        functools.partial(regroup_kernel, sizes),
-        grid_spec=pltpu.PrefetchScalarGridSpec(
-            num_scalar_prefetch=1,
-            grid=(owners,),
-            in_specs=[pl.BlockSpec((spill_height, LANES), lambda o, at: (0, 0))] * columns,
-            out_specs=[pl.BlockSpec(shape, lambda o, at: (0, 0)) for shape in outs],
-            scratch_shapes=[
-                pltpu.VMEM((columns * sizes.spill, part), jnp.bfloat16),
-                pltpu.VMEM((16, columns * sizes.spill), jnp.float32),
-                pltpu.VMEM((sizes.second, columns * sizes.spill), jnp.bfloat16),
-            ],
-        ),
-        out_shape=[jax.ShapeDtypeStruct(shape, jnp.bfloat16) for shape in outs],
-        compiler_params=params,
-        name="regroup",
-    )(at, *spills)
+    smem, vmem = pl.BlockSpec(memory_space=pltpu.SMEM), pl.BlockSpec(memory_space=pltpu.VMEM)
+
+    def regroup(spills, start, count, heights, name):
+        shape = jax.ShapeDtypeStruct((heights + count, part), jnp.bfloat16)
+        return pl.pallas_call(
+            functools.partial(regroup_kernel, sizes, start, count, heights),
+            in_specs=[smem] + [vmem] * columns,
+            out_specs=[vmem] * owners,
+            out_shape=[shape] * owners,
+            scratch_shapes=[pltpu.VMEM((columns * sizes.spill, part), jnp.bfloat16)],
+            compiler_params=params,
+            name=name,
+        )(at, *spills)
 
     def swap(arrays):
         return arrays[:1] + [
@@ -496,15 +480,13 @@
             for n in range(1, owners)
         ]
 
-    parts = list(parts)
-    bases, rests = swap(parts[:owners]), parts[owners:]
-
-    sources = min(devices, 1024 // sizes.rows)
+    bases = swap(list(regroup(spills, 0, sizes.base, sizes.base_notes, "regroup")))
+
+    sources = min(devices, 1 << (1024 // sizes.rows).bit_length() - 1)
     chunks = devices // sources
     copies = devices if devices <= 64 else 1
     height = 8 * sizes.pages
     flux_spec = pl.BlockSpec((sizes.hours, sizes.tiles, part), lambda i, at: (0, 0, at[1]))
-    base_specs = [pl.BlockSpec((base_height, part), lambda i, at: (0, 0))] * owners
     early, level, feet_first, read_first = pl.pallas_call(
         functools.partial(forward_first_kernel, sizes),
         grid_spec=pltpu.PrefetchScalarGridSpec(
@@ -532,33 +514,36 @@
         name="forward_first",
     )(at, flux, got, got)
 
-    smem, vmem = pl.BlockSpec(memory_space=pltpu.SMEM), pl.BlockSpec(memory_space=pltpu.VMEM)
     late_flux = lax.optimization_barrier((flux, mine))[0]
     own_flux = lax.dynamic_slice_in_dim(late_flux, lax.axis_index("obs") * part, part, axis=2)
 
-    def forward_second(own_flux, before, bases, rests, more):
+    def forward_second(own_flux, before, parts, heights, name):
         return pl.pallas_call(
-            functools.partial(forward_second_kernel, sizes, more > 0),
-            in_specs=[smem] + [vmem] * (2 + len(bases) + len(rests)),
+            functools.partial(forward_second_kernel, sizes, heights),
+            in_specs=[smem] + [vmem] * (2 + len(parts)),
             out_specs=(vmem, vmem),
             out_shape=(
                 jax.ShapeDtypeStruct((copies, height, LANES), jnp.float32),
-                jax.ShapeDtypeStruct((8, owners * (more or sizes.base)), jnp.float32),
+                jax.ShapeDtypeStruct((8, owners * (parts[0].shape[0] - heights)), jnp.float32),
             ),
             compiler_params=params,
-            name="forward_more" if more else "forward_second",
-        )(at, own_flux, before, *bases, *rests)
-
-    sums, read_second = forward_second(own_flux, early[None], bases, [], 0)
+            name=name,
+        )(at, own_flux, before, *parts)
+
+    sums, read_second = forward_second(
+        own_flux, early[None], bases, sizes.base_notes, "forward_second"
+    )
+    late_spills = lax.optimization_barrier((spills, early))[0]
+    rests = list(regroup(late_spills, sizes.base, sizes.rest, sizes.rest_notes, "regroup_rest"))
     kept = (feet_first, read_first, read_second)
 
-    def finish(sixteenths):
-        more = sizes.second * sixteenths // 16
-
+    def finish(more):
         def run(own_flux, kept, sums, bases, rests, at):
             if more:
-                rests = swap([rest[:more] for rest in rests])
-                sums, read_more = forward_second(own_flux, sums, bases, rests, more)
+                rests = swap([rest[: sizes.rest_notes + more] for rest in rests])
+                sums, read_more = forward_second(
+                    own_flux, sums, rests, sizes.rest_notes, "forward_more"
+                )
                 rests.append(read_more)
             else:
                 rests = []
@@ -585,7 +570,7 @@
         return run
 
     modeled, gradient = lax.switch(
-        level[0, 0], [finish(n) for n in REST], own_flux, kept, sums, bases, rests, at
+        level[0, 0], [finish(n) for n in sizes.levels], own_flux, kept, sums, bases, rests, at
     )
     return modeled.T, gradient.transpose(1, 0, 2)
 

time: 105 us -> 100 us (0.952)
  waiting for transfers between devices: 44 us -> 36.3 us
  Pallas kernels: 21.4 us -> 23.6 us
    ppermute x3, waiting for transfers between devices: 12.4 us -> 8.49 us  [swap(): lax.ppermute(arrays[n], 'flux', [(i, i ^ n) for i in range(owners)])]
    all_to_all x1, waiting for transfers between devices: 3.09 us -> 0.01 us  [shards(): lax.all_to_all(send.reshape(devices, first_height, LANES), both, split_ax...]
    pallas_call x2 -> x3, Pallas kernels: 8.07 us -> 8.98 us  [the longest x2 6.49 us: regroup(): pl.pallas_call(functools.partial(regroup_kernel, sizes, start, count, hei...]
  transfers between devices with their start and end apart: 11 -> 11, of which waited for: 6 -> 6; matrix products, arithmetic and copies ran while one was open for 2% -> 3% of each run, Pallas kernels for 9% -> 11%
where the time goes in v3:
time: 100 us; the launch traced here: 99.9 us
  waiting for transfers between devices  36.3 us (36%)
  Pallas kernels  23.6 us (24%)
  starting transfers between devices  19.7 us (20%)
  blocking collectives  15.9 us (16%)
  local copies, waits for them, and re-layouts  2.53 us (3%)
  between operations  1.54 us (2%)
    ppermute x7, waiting for transfers between devices, shards(): lax.ppermute(spills[d], 'obs', [(i, i ^ d) for i in range(columns)])  27.8 us
    all_to_all x1, blocking collectives, run(): sums = lax.all_to_all(sums, both, split_axis=0, concat_axis=0, tiled=True)  15.9 us
    ppermute x3, waiting for transfers between devices, swap(): lax.ppermute(arrays[n], 'flux', [(i, i ^ n) for i in range(owners)])  8.49 us
    all_to_all x1, starting transfers between devices, shards(): lax.all_to_all(send.reshape(devices, first_height, LANES), both, split_ax...  7.28 us
    ppermute x7, starting transfers between devices, shards(): lax.ppermute(spills[d], 'obs', [(i, i ^ d) for i in range(columns)])  6.76 us
    pallas_call x2, Pallas kernels, regroup(): pl.pallas_call(functools.partial(regroup_kernel, sizes, start, count, hei...  6.49 us
    ppermute x3, starting transfers between devices, swap(): lax.ppermute(arrays[n], 'flux', [(i, i ^ n) for i in range(owners)])  5.67 us
    pallas_call x1, Pallas kernels, run(): pl.pallas_call(functools.partial(adjoint_kernel, sizes), in_specs=[smem]...  5.65 us
  transfers between devices with their start and end apart: 11, of which 6 were waited for; matrix products, arithmetic and copies ran while one was open for 3% of the time, Pallas kernels for 11%

profile of v3, /device:TPU:0, one launch (start us, length us, event | category | flops | bytes accessed | tf_op | source)
XLA Modules:
  0.0 99.9 jit_solution(269661901317573360)
XLA Ops:
  0.6 0.1 pad_add_fusion.at_ref
  0.7 4.2 %pack.1 = (bf16[4,8,232,128]{3,2,1,0:T(8,128)(2,1)}, bf16[608,128]{1,0:T(8,128)(2,1)}, bf16[608,128]{1,0:T(8,128)(2,1)}, bf16[608,128]{1,0:T(8,128)(2,1)}, bf16[...) custom-call(s32[3]{0:T(128)S(1)} %pad_add_fusion.at_ref, ...), custom_call_target="tpu_custom_call" | custom-call | tf_op jit(solution)/shard_map/pack/pallas_call | solution.py:430
  4.9 0.0 copy-start.7
  4.9 0.0 copy-start.6
  4.9 0.0 copy-start.5
  4.9 0.0 copy-start.4
  5.0 0.0 copy-start
  5.0 7.3 %all-to-all-start.4 = ((bf16[32,232,128]{2,1,0:T(8,128)(2,1)}), bf16[32,232,128]{2,1,0:T(8,128)(2,1)S(1)}, u32[]{:S(2)}, u32[]{:S(2)}) async-start(bf16[32,232,128]{2,1,0:T(8,128)(2,1)} %bitcast.18), calls=%async_computation.4 | async-start | bytes 3801088 | tf_op jit(solution)/shard_map/all_to_all | solution.py:455
  12.3 0.0 copy-done.7
  12.3 0.3 collective-permute-start.9
  12.6 0.0 copy-done.6
  12.6 1.7 %collective-permute-start.10 = (bf16[608,128]{1,0:T(8,128)(2,1)S(1)}, bf16[608,128]{1,0:T(8,128)(2,1)S(1)}, u32[]{:S(2)}, u32[]{:S(2)}) collective-permute-start(bf16[608,128]{1,0:T(8,128)(2,1)S(1)} %copy-done.6), channel_id=1, source_target_pairs={{0,2},{1,3},{2,0},{3,1},{4,6},{5,7},{6,4},{7,5},{8,10},{9,11},{10,... | collective-permute-start | bytes 466952 | tf_op jit(solution)/shard_map/ppermute | solution.py:460
  14.3 0.0 collective-permute-start.11
  14.3 1.7 %collective-permute-start.12 = (bf16[608,128]{1,0:T(8,128)(2,1)}, bf16[608,128]{1,0:T(8,128)(2,1)S(1)}, u32[]{:S(2)}, u32[]{:S(2)}) collective-permute-start(bf16[608,128]{1,0:T(8,128)(2,1)} %get-tuple-element.203), channel_id=1, source_target_pairs={{0,4},{1,5},{2,6},{3,7},{4,0},{5,1},{6,2},{7,3},{8,12},{9,13},{10,... | collective-permute-start | bytes 466952 | tf_op jit(solution)/shard_map/ppermute | solution.py:460
  16.0 0.1 collective-permute-start.13
  16.1 0.0 collective-permute-done.9.refs_1_
  16.1 0.0 copy-done.5
  16.1 2.6 %collective-permute-start.14 = (bf16[608,128]{1,0:T(8,128)(2,1)S(1)}, bf16[608,128]{1,0:T(8,128)(2,1)S(1)}, u32[]{:S(2)}, u32[]{:S(2)}) collective-permute-start(bf16[608,128]{1,0:T(8,128)(2,1)S(1)} %copy-done.5), channel_id=1, source_target_pairs={{0,6},{1,7},{2,4},{3,5},{4,2},{5,3},{6,0},{7,1},{8,14},{9,15},{10,... | collective-permute-start | bytes 466952 | tf_op jit(solution)/shard_map/ppermute | solution.py:460
  18.7 12.4 %collective-permute-done.10.refs_2_ = bf16[608,128]{1,0:T(8,128)(2,1)S(1)} collective-permute-done((bf16[608,128]{1,0:T(8,128)(2,1)S(1)}, bf16[608,128]{1,0:T(8,128)(2,1)S(1)}, u32[]{:S(2)}, u32[]{:S(2)}) %collective-permute-start.10) | collective-permute-done | bytes 155680 | tf_op jit(solution)/shard_map/ppermute | solution.py:460
  31.0 0.0 copy-done.4
  31.0 0.4 collective-permute-start.15
  31.4 6.4 %collective-permute-done.11.refs_3_ = bf16[608,128]{1,0:T(8,128)(2,1)S(1)} collective-permute-done((bf16[608,128]{1,0:T(8,128)(2,1)}, bf16[608,128]{1,0:T(8,128)(2,1)S(1)}, u32[]{:S(2)}, u32[]{:S(2)}) %collective-permute-start.11) | collective-permute-done | bytes 155680 | tf_op jit(solution)/shard_map/ppermute | solution.py:460
  37.8 0.0 collective-permute-done.12.refs_4_
  37.8 0.0 collective-permute-done.13.refs_5_
  37.8 6.3 %collective-permute-done.14.refs_6_ = bf16[608,128]{1,0:T(8,128)(2,1)S(1)} collective-permute-done((bf16[608,128]{1,0:T(8,128)(2,1)S(1)}, bf16[608,128]{1,0:T(8,128)(2,1)S(1)}, u32[]{:S(2)}, u32[]{:S(2)}) %collective-permute-start.14) | collective-permute-done | bytes 155680 | tf_op jit(solution)/shard_map/ppermute | solution.py:460
  44.1 2.7 %collective-permute-done.15.refs_7_ = bf16[608,128]{1,0:T(8,128)(2,1)S(1)} collective-permute-done((bf16[608,128]{1,0:T(8,128)(2,1)S(1)}, bf16[608,128]{1,0:T(8,128)(2,1)S(1)}, u32[]{:S(2)}, u32[]{:S(2)}) %collective-permute-start.15) | collective-permute-done | bytes 155680 | tf_op jit(solution)/shard_map/ppermute | solution.py:460
  46.8 0.0 copy-done
  46.8 3.1 %regroup.1 = (bf16[264,512]{1,0:T(8,128)(2,1)}, bf16[264,512]{1,0:T(8,128)(2,1)}, bf16[264,512]{1,0:T(8,128)(2,1)}, bf16[264,512]{1,0:T(8,128)(2,1)S(1)}) custom-call(s32[3]{0:T(128)S(1)} %pad_add_fusion.at_ref, bf16[608,128]{1,0:T(8,128)(2,1)S(1)} %copy-done, bf16[608,128]{1,0:T(8,128)(2,1)S(1)} %collective-permute-done.9.refs_1_, ...), custom_call_target="tpu_custom_call" | custom-call | tf_op jit(solution)/shard_map/regroup/pallas_call | solution.py:467
  50.0 3.3 %collective-permute-start.16 = (bf16[264,512]{1,0:T(8,128)(2,1)}, bf16[264,512]{1,0:T(8,128)(2,1)}, u32[]{:S(2)}, u32[]{:S(2)}) collective-permute-start(bf16[264,512]{1,0:T(8,128)(2,1)} %get-tuple-element.208), channel_id=1, source_target_pairs={{0,8},{8,0},{16,24},{24,16},{1,9},{9,1},{17,25},{25,17},{2,10},{10... | collective-permute-start | bytes 811016 | tf_op jit(solution)/shard_map/ppermute | solution.py:479
  53.3 1.8 %collective-permute-start.17 = (bf16[264,512]{1,0:T(8,128)(2,1)}, bf16[264,512]{1,0:T(8,128)(2,1)}, u32[]{:S(2)}, u32[]{:S(2)}) collective-permute-start(bf16[264,512]{1,0:T(8,128)(2,1)} %get-tuple-element.209), channel_id=1, source_target_pairs={{0,16},{8,24},{16,0},{24,8},{1,17},{9,25},{17,1},{25,9},{2,18},{10... | collective-permute-start | bytes 811016 | tf_op jit(solution)/shard_map/ppermute | solution.py:479
  55.1 0.6 collective-permute-start.18
  55.6 2.0 %constant_dynamic-slice_fusion.flux_ref = bf16[5,128,512]{2,1,0:T(8,128)(2,1)} fusion(bf16[5,128,4096]{2,1,0:T(8,128)(2,1)} %bitcast.15, s32[]{:T(128)S(6)} %select_n.3), kind=kLoop, calls=%fused_computation.1 | loop fusion | bytes 1310724 | tf_op jit(solution)/shard_map/dynamic_slice | solution.py:518
  57.6 0.0 all-to-all-done.4.got_ref.all_ref
  57.6 4.8 %forward_first.1 = (f32[8,128]{1,0:T(8,128)S(1)}, s32[8,128]{1,0:T(8,128)S(1)}, bf16[1792,512]{1,0:T(8,128)(2,1)}, f32[8,1792]{1,0:T(8,128)S(1)}) custom-call(s32[3]{0:T(128)S(1)} %pad_add_fusion.at_ref, bf16[5,128,4096]{2,1,0:T(8,128)(2,1)} %bitcast.16, bf16[32,232,128]{2,1,0:T(8,128)(2,1)S(1)} %all-to-all-done.4.got_ref.all_ref, ...), custom_call_target="tpu_custom_call" | custom-call | tf_op jit(solution)/shard_map/forward_first/pallas_call | solution.py:490
  62.4 0.5 slice.27
  63.6 3.3 %regroup_rest.1 = (bf16[328,512]{1,0:T(8,128)(2,1)S(1)}, bf16[328,512]{1,0:T(8,128)(2,1)S(1)}, bf16[328,512]{1,0:T(8,128)(2,1)S(1)}, bf16[328,512]{1,0:T(8,128)(2,1)S(1)}) custom-call(s32[3]{0:T(128)S(1)} %pad_add_fusion.at_ref, bf16[608,128]{1,0:T(8,128)(2,1)S(1)} %copy-done, bf16[608,128]{1,0:T(8,128)(2,1)S(1)} %collective-permute-done.9.refs_1_, ...), custom_call_target="tpu_custom_call" | custom-call | tf_op jit(solution)/shard_map/regroup_rest/pallas_call | solution.py:467
  66.9 0.8 collective-permute-done.16.refs_1_
  67.7 7.7 %collective-permute-done.17.refs_2_ = bf16[264,512]{1,0:T(8,128)(2,1)} collective-permute-done((bf16[264,512]{1,0:T(8,128)(2,1)}, bf16[264,512]{1,0:T(8,128)(2,1)}, u32[]{:S(2)}, u32[]{:S(2)}) %collective-permute-start.17) | collective-permute-done | bytes 270368 | tf_op jit(solution)/shard_map/ppermute | solution.py:479
  75.4 0.0 collective-permute-done.18.refs_3_
  75.4 2.5 %forward_second.1 = (f32[32,8,128]{2,1,0:T(8,128)S(1)}, f32[8,1024]{1,0:T(8,128)S(1)}) custom-call(s32[3]{0:T(128)S(1)} %pad_add_fusion.at_ref, bf16[5,128,512]{2,1,0:T(8,128)(2,1)} %constant_dynamic-slice_fusion.flux_ref, f32[1,8,128]{2,1,0:T(8,128)S(1)} %bitcast.14, bf16[264,512]{1,0:T(8,128)(2,1)} %get-tuple-element.207.refs_0_, ...), custom_call_target="tpu_custom_call" | custom-call | tf_op jit(solution)/shard_map/forward_second/pallas_call | solution.py:521
  77.9 21.8 %conditional.1 = ((f32[4,8]{1,0:T(4,128)}, f32[5,128,512]{2,1,0:T(8,128)})) conditional(s32[]{:T(128)} %bitcast.10, (f32[32,8,128]{2,1,0:T(8,128)S(1)}, s32[3]{0:T(128)S(1)}, bf16[1792,512]{1,0:T(8,128)(2,1)}, f32[8,1792]{1,0:T(8,128)S(1)}, f32[8,1024]{1,0:T(8,128)S(1)}, /*index=5*/bf16[264,512]{1,0:T(8,128)(2,1)}, ...), branch_computations={%region_0.0_spmd, %region_1.0_spmd, %region_2.0_spmd, %region_3.0_... | conditional | bytes 11632796 | solution.py:572
  77.9 15.9 %all_to_all.21.sums_ref = f32[32,8,128]{2,1,0:T(8,128)S(1)} all-to-all(f32[32,8,128]{2,1,0:T(8,128)S(1)} %get-tuple-element.103), channel_id=1, replica_groups=mesh['flux'=4,'obs'=8] {'flux','obs'}, dimensions={0} | all-to-all | bytes 262144 | tf_op jit(solution)/shard_map/cond/branch_0_fun/all_to_all | solution.py:551
  93.9 5.7 %adjoint.4 = (f32[4,8]{1,0:T(4,128)}, f32[5,128,512]{2,1,0:T(8,128)}) custom-call(s32[3]{0:T(128)S(1)} %get-tuple-element.102.at_ref, f32[32,8,128]{2,1,0:T(8,128)S(1)} %all_to_all.21.sums_ref, bf16[1792,512]{1,0:T(8,128)(2,1)} %get-tuple-element.104.feet_ref, f32[8,1792]{1,0:T(8,128)S(1)} %get-tuple-element.105.read_ref, ...), custom_call_target="tpu_custom_call" | custom-call | tf_op jit(solution)/shard_map/cond/branch_0_fun/adjoint/pallas_call | solution.py:554
Async XLA Ops:
  4.9 7.3 %copy-start.7 = (bf16[608,128]{1,0:T(8,128)(2,1)S(1)}, bf16[608,128]{1,0:T(8,128)(2,1)}, u32[]{:S(2)}) copy-start(bf16[608,128]{1,0:T(8,128)(2,1)} %get-tuple-element.200) | copy-start | bytes 466948
  4.9 7.7 %copy-start.6 = (bf16[608,128]{1,0:T(8,128)(2,1)S(1)}, bf16[608,128]{1,0:T(8,128)(2,1)}, u32[]{:S(2)}) copy-start(bf16[608,128]{1,0:T(8,128)(2,1)} %get-tuple-element.201) | copy-start | bytes 466948
  4.9 11.1 %copy-start.5 = (bf16[608,128]{1,0:T(8,128)(2,1)S(1)}, bf16[608,128]{1,0:T(8,128)(2,1)}, u32[]{:S(2)}) copy-start(bf16[608,128]{1,0:T(8,128)(2,1)} %get-tuple-element.205) | copy-start | bytes 466948
  4.9 26.1 %copy-start.4 = (bf16[608,128]{1,0:T(8,128)(2,1)S(1)}, bf16[608,128]{1,0:T(8,128)(2,1)}, u32[]{:S(2)}) copy-start(bf16[608,128]{1,0:T(8,128)(2,1)} %get-tuple-element.206) | copy-start | bytes 466948
  5.0 41.9 %copy-start = (bf16[608,128]{1,0:T(8,128)(2,1)S(1)}, bf16[608,128]{1,0:T(8,128)(2,1)}, u32[]{:S(2)}) copy-start(bf16[608,128]{1,0:T(8,128)(2,1)} %get-tuple-element.215.refs_0_) | copy-start | bytes 466948
  5.0 52.7 %all-to-all-start.4 = ((bf16[32,232,128]{2,1,0:T(8,128)(2,1)}), bf16[32,232,128]{2,1,0:T(8,128)(2,1)S(1)}, u32[]{:S(2)}, u32[]{:S(2)}) async-start(bf16[32,232,128]{2,1,0:T(8,128)(2,1)} %bitcast.18), calls=%async_computation.4 | async-start | bytes 3801088 | tf_op jit(solution)/shard_map/all_to_all | solution.py:455
  12.3 3.8 %collective-permute-start.9 = (bf16[608,128]{1,0:T(8,128)(2,1)S(1)}, bf16[608,128]{1,0:T(8,128)(2,1)S(1)}, u32[]{:S(2)}, u32[]{:S(2)}) collective-permute-start(bf16[608,128]{1,0:T(8,128)(2,1)S(1)} %copy-done.7), channel_id=1, source_target_pairs={{0,1},{1,0},{2,3},{3,2},{4,5},{5,4},{6,7},{7,6},{8,9},{9,8},{10,11... | collective-permute-start | bytes 466952 | tf_op jit(solution)/shard_map/ppermute | solution.py:460
  12.6 18.5 %collective-permute-start.10 = (bf16[608,128]{1,0:T(8,128)(2,1)S(1)}, bf16[608,128]{1,0:T(8,128)(2,1)S(1)}, u32[]{:S(2)}, u32[]{:S(2)}) collective-permute-start(bf16[608,128]{1,0:T(8,128)(2,1)S(1)} %copy-done.6), channel_id=1, source_target_pairs={{0,2},{1,3},{2,0},{3,1},{4,6},{5,7},{6,4},{7,5},{8,10},{9,11},{10,... | collective-permute-start | bytes 466952 | tf_op jit(solution)/shard_map/ppermute | solution.py:460
  14.3 23.6 %collective-permute-start.11 = (bf16[608,128]{1,0:T(8,128)(2,1)}, bf16[608,128]{1,0:T(8,128)(2,1)S(1)}, u32[]{:S(2)}, u32[]{:S(2)}) collective-permute-start(bf16[608,128]{1,0:T(8,128)(2,1)} %get-tuple-element.202), channel_id=1, source_target_pairs={{0,3},{1,2},{2,1},{3,0},{4,7},{5,6},{6,5},{7,4},{8,11},{9,10},{10,... | collective-permute-start | bytes 466952 | tf_op jit(solution)/shard_map/ppermute | solution.py:460
  14.3 23.6 %collective-permute-start.12 = (bf16[608,128]{1,0:T(8,128)(2,1)}, bf16[608,128]{1,0:T(8,128)(2,1)S(1)}, u32[]{:S(2)}, u32[]{:S(2)}) collective-permute-start(bf16[608,128]{1,0:T(8,128)(2,1)} %get-tuple-element.203), channel_id=1, source_target_pairs={{0,4},{1,5},{2,6},{3,7},{4,0},{5,1},{6,2},{7,3},{8,12},{9,13},{10,... | collective-permute-start | bytes 466952 | tf_op jit(solution)/shard_map/ppermute | solution.py:460
  16.0 21.9 %collective-permute-start.13 = (bf16[608,128]{1,0:T(8,128)(2,1)}, bf16[608,128]{1,0:T(8,128)(2,1)S(1)}, u32[]{:S(2)}, u32[]{:S(2)}) collective-permute-start(bf16[608,128]{1,0:T(8,128)(2,1)} %get-tuple-element.204), channel_id=1, source_target_pairs={{0,5},{1,4},{2,7},{3,6},{4,1},{5,0},{6,3},{7,2},{8,13},{9,12},{10,... | collective-permute-start | bytes 466952 | tf_op jit(solution)/shard_map/ppermute | solution.py:460
  16.1 28.0 %collective-permute-start.14 = (bf16[608,128]{1,0:T(8,128)(2,1)S(1)}, bf16[608,128]{1,0:T(8,128)(2,1)S(1)}, u32[]{:S(2)}, u32[]{:S(2)}) collective-permute-start(bf16[608,128]{1,0:T(8,128)(2,1)S(1)} %copy-done.5), channel_id=1, source_target_pairs={{0,6},{1,7},{2,4},{3,5},{4,2},{5,3},{6,0},{7,1},{8,14},{9,15},{10,... | collective-permute-start | bytes 466952 | tf_op jit(solution)/shard_map/ppermute | solution.py:460
  31.0 15.8 %collective-permute-start.15 = (bf16[608,128]{1,0:T(8,128)(2,1)S(1)}, bf16[608,128]{1,0:T(8,128)(2,1)S(1)}, u32[]{:S(2)}, u32[]{:S(2)}) collective-permute-start(bf16[608,128]{1,0:T(8,128)(2,1)S(1)} %copy-done.4), channel_id=1, source_target_pairs={{0,7},{1,6},{2,5},{3,4},{4,3},{5,2},{6,1},{7,0},{8,15},{9,14},{10,... | collective-permute-start | bytes 466952 | tf_op jit(solution)/shard_map/ppermute | solution.py:460
  50.0 17.8 %collective-permute-start.16 = (bf16[264,512]{1,0:T(8,128)(2,1)}, bf16[264,512]{1,0:T(8,128)(2,1)}, u32[]{:S(2)}, u32[]{:S(2)}) collective-permute-start(bf16[264,512]{1,0:T(8,128)(2,1)} %get-tuple-element.208), channel_id=1, source_target_pairs={{0,8},{8,0},{16,24},{24,16},{1,9},{9,1},{17,25},{25,17},{2,10},{10... | collective-permute-start | bytes 811016 | tf_op jit(solution)/shard_map/ppermute | solution.py:479
  53.3 22.1 %collective-permute-start.17 = (bf16[264,512]{1,0:T(8,128)(2,1)}, bf16[264,512]{1,0:T(8,128)(2,1)}, u32[]{:S(2)}, u32[]{:S(2)}) collective-permute-start(bf16[264,512]{1,0:T(8,128)(2,1)} %get-tuple-element.209), channel_id=1, source_target_pairs={{0,16},{8,24},{16,0},{24,8},{1,17},{9,25},{17,1},{25,9},{2,18},{10... | collective-permute-start | bytes 811016 | tf_op jit(solution)/shard_map/ppermute | solution.py:479
  55.1 20.4 %collective-permute-start.18 = (bf16[264,512]{1,0:T(8,128)(2,1)S(1)}, bf16[264,512]{1,0:T(8,128)(2,1)}, u32[]{:S(2)}, u32[]{:S(2)}) collective-permute-start(bf16[264,512]{1,0:T(8,128)(2,1)S(1)} %get-tuple-element.210), channel_id=1, source_target_pairs={{0,24},{8,16},{16,8},{24,0},{1,25},{9,17},{17,9},{25,1},{2,26},{10... | collective-permute-start | bytes 811016 | tf_op jit(solution)/shard_map/ppermute | solution.py:479
